TPU v7x, 128 devices: a whole 4x4x4 slice. The times are simulated.
128 devices in a mesh: groups: 32 (over y, x, core), block: 4 (over z).
Axes of the slice: x: 4, y: 4, z: 4, core: 2. Of those that a mesh axis runs over, the one named last changes fastest.
Arguments:
- embeddings: bfloat16 [65536, 768], P(('groups', 'block'))
- cluster_ids: int32 [65536], P(('groups', 'block')), may hold values from 0 to 511, as said below
Outputs:
- similarity: float32 [65536], P(('groups', 'block'))
Inputs may be any that keep to these rules, and one draw needn't show every extreme that they name: `cluster_ids`: clusters 16 * g to 16 * g + 15 form owner group g. Among the 512 rows of one device at most 64 lie in one group's clusters, and one group gets exactly 64 rows from every device.
All inputs are finite; a program needn't handle non-finite values.
Results may differ from a plain program's by a relative error of at most 0.00053.
Values may be sent and summed in bfloat16 or wider, within the bound.
No kernel may reach another device: no remote copies, remote signals or barrier semaphores. Data moves between devices by JAX's collectives and lax.ppermute only.
A program may use at most 64 MiB of HBM per device.

v0:
```python
import jax
import jax.numpy as jnp
from jax import lax
from jax.sharding import PartitionSpec as P

CL_GRP = 16


def pair_max(left_rows, left_ids, left_pos, right_rows, right_ids, right_pos):
    left_total = left_rows.shape[0]
    width = left_rows.shape[1]
    left_step = min(512, left_total)
    left_count = left_total // left_step
    left_rows_b = left_rows.reshape(left_count, left_step, width)
    left_ids_b = left_ids.reshape(left_count, left_step)
    left_pos_b = left_pos.reshape(left_count, left_step)

    def left_turn(column_carry, left_tuple):
        part_rows, part_ids, part_pos = left_tuple
        scores = lax.dot_general(
            part_rows, right_rows, (((1,), (1,)), ((), ())), preferred_element_type=jnp.float32
        )
        matches = (
            (part_ids[:, None] == right_ids[None, :])
            & (part_ids[:, None] >= 0)
            & (part_pos[:, None] != right_pos[None, :])
        )
        masked = jnp.where(matches, scores, -1.0)
        return (jnp.maximum(column_carry, jnp.max(masked, axis=0)), jnp.max(masked, axis=1))

    start_columns = jnp.full((right_rows.shape[0],), -1.0, jnp.float32)
    column_best, row_best = lax.scan(
        left_turn, start_columns, (left_rows_b, left_ids_b, left_pos_b)
    )
    return (row_best.reshape(-1), column_best)


def body(embeddings, cluster_ids):
    groups = lax.axis_size("groups")
    local_rows = embeddings.shape[0]
    row_width = embeddings.shape[1]
    capacity = 4 * local_rows // groups
    widened = embeddings.astype(jnp.float32)
    normed = (
        widened * lax.rsqrt(jnp.sum(widened * widened, axis=1, keepdims=True) + 1e-06)
    ).astype(jnp.bfloat16)
    owner_group = cluster_ids // CL_GRP
    one_hot = (owner_group[:, None] == jnp.arange(groups, dtype=jnp.int32)[None, :]).astype(
        jnp.int32
    )
    slot_index = jnp.sum(jnp.cumsum(one_hot, axis=0) * one_hot, axis=1) - 1
    flat_slot = owner_group * capacity + slot_index
    placement = jnp.arange(groups * capacity, dtype=jnp.int32)[:, None] == flat_slot[None, :]
    outgoing = jnp.dot(
        placement.astype(jnp.bfloat16), normed, preferred_element_type=jnp.float32
    ).astype(jnp.bfloat16)
    outgoing = outgoing.reshape(groups, capacity, row_width)
    outgoing_ids = jnp.max(jnp.where(placement, cluster_ids[None, :], -1), axis=1).reshape(
        groups, capacity
    )
    arrived, arrived_ids = (
        lax.all_to_all(outgoing, "groups", split_axis=0, concat_axis=0, tiled=True),
        lax.all_to_all(outgoing_ids, "groups", split_axis=0, concat_axis=0, tiled=True),
    )
    received = arrived.reshape(groups * capacity, row_width)
    received_ids = arrived_ids.reshape(groups * capacity)
    held_rows = received.shape[0]
    local_pos = jnp.arange(held_rows, dtype=jnp.int32)
    own_pos = local_pos + lax.axis_index("block") * held_rows
    piece_rows = lax.all_gather(received, "block", axis=0, tiled=True)
    piece_ids = lax.all_gather(received_ids, "block", axis=0, tiled=True)
    piece_pos = jnp.arange(piece_rows.shape[0], dtype=jnp.int32)
    row_best, unused_columns = pair_max(
        received, received_ids, own_pos, piece_rows, piece_ids, piece_pos
    )
    best = jnp.maximum(jnp.full((held_rows,), -1.0, jnp.float32), row_best)
    returned = lax.all_to_all(
        best.reshape(groups, capacity), "groups", split_axis=0, concat_axis=0, tiled=True
    )
    returned_flat = returned.reshape(groups * capacity)
    return jnp.max(jnp.where(placement, returned_flat[:, None], -2.0), axis=0)


def solution(mesh):
    in_specs = (P(("groups", "block"), None), P(("groups", "block")))
    out_specs = P(("groups", "block"))
    return jax.shard_map(body, mesh=mesh, in_specs=in_specs, out_specs=out_specs, check_vma=False)
```

profile of v0, /device:TPU:0, one launch (start us, length us, event | category | flops | bytes accessed | tf_op | source)
XLA Modules:
  0.0 254.5 jit_solution(5008057855116917173)
XLA Ops:
  6.5 0.7 fusion.19
  7.2 0.7 add_select_fusion
  7.9 1.2 reduce-window.6
  9.5 0.7 add_add_fusion.1
  10.2 1.4 fusion.9
  11.5 3.2 %fusion.7 = bf16[2048,768]{1,0:T(8,128)(2,1)S(1)} fusion(s32[512]{0:T(512)S(1)} %add_add_fusion.1, bf16[512,768]{1,0:T(8,128)(2,1)} %param.4, f32[512]{0:T(512)S(1)} %add_rsqrt_fusion), kind=kOutput, calls=%fused_computation.14 | convolution fusion | flops 1614413824 | bytes 3936256 | tf_op jit(solution)/shard_map/dot_general | solution.py:54
  14.7 47.1 %all_to_all.20 = bf16[32,64,768]{2,1,0:T(8,128)(2,1)} all-to-all(bf16[32,64,768]{2,1,0:T(8,128)(2,1)S(1)} %bitcast.40), channel_id=1, replica_groups=mesh['groups'=32,'block'=4] {'groups'}, dimensions={0} | all-to-all | bytes 6291456 | tf_op jit(solution)/shard_map/all_to_all | solution.py:62
  61.9 0.6 select_reduce_fusion.2
  62.5 0.7 all_to_all.13
  63.2 3.8 %all-to-all-start = ((s32[32,1,64]{2,1,0:T(1,128)}), s32[32,1,64]{2,1,0:T(1,128)S(1)}, u32[]{:S(2)}, u32[]{:S(2)}) async-start(s32[32,1,64]{2,1,0:T(1,128)} %all_to_all.13), calls=%async_computation | async-start | bytes 32768 | tf_op jit(solution)/shard_map/all_to_all | solution.py:63
  67.0 7.3 %all-to-all-done = s32[32,1,64]{2,1,0:T(1,128)S(1)} async-done(((s32[32,1,64]{2,1,0:T(1,128)}), s32[32,1,64]{2,1,0:T(1,128)S(1)}, u32[]{:S(2)}, u32[]{:S(2)}) %all-to-all-start) | async-done | bytes 8224 | tf_op jit(solution)/shard_map/all_to_all | solution.py:63
  74.4 0.5 broadcast.75
  75.0 0.7 reduce.10
  75.7 13.2 %all_gather.6 = s32[8192]{0:T(1024)S(1)} all-gather(s32[2048]{0:T(1024)S(1)} %reshape.74), channel_id=1, replica_groups=mesh['groups'=32,'block'=4] {'block'}, dimensions={0}, use_global_device_ids=true | all-gather | bytes 40960 | tf_op jit(solution)/shard_map/all_gather | solution.py:71
  88.9 90.7 %all-gather.2.cloned.1.call-done = bf16[8192,768]{1,0:T(8,128)(2,1)} async-done(((bf16[2048,768]{1,0:T(8,128)(2,1)}), bf16[8192,768]{1,0:T(8,128)(2,1)}) %all-gather.2.cloned.1.call-update) | async-done | bytes 12582928 | tf_op jit(solution)/shard_map/all_gather | solution.py:70
  179.6 51.3 %while.11 = (s32[]{:T(128)}, f32[4,512]{1,0:T(4,128)S(1)}, s32[4,512]{1,0:T(4,128)S(1)}, s32[8192]{0:T(1024)S(1)}, s32[4,512]{1,0:T(4,128)S(1)}, /*index=5*/bf16...) while((s32[]{:T(128)}, f32[4,512]{1,0:T(4,128)S(1)}, ...), condition=%wide.region_7.8_spmd.clone, body=%wide.region_5.7_spmd.clone.sunk | while | flops 6467616768 | bytes 13424229 | solution.py:32
  179.6 12.7 %select_reduce_fusion.4 = f32[512]{0:T(512)S(1)} fusion(bf16[8192,768]{1,0:T(8,128)(2,1)} %get-tuple-element.151, s32[512]{0:T(512)S(1)} %bitcast.44, s32[8192]{0:T(1024)S(1)} %get-tuple-element.148, s32[512]{0:T(512)S(1)} %bitcast.42, pred[512]{0:T(512)(128)(4,1)S(1)} %broadcast_compare_fusion.2, bf16[4,512,768]{2,1,0:T(8,128)(2,1)} %get-tuple-element.150, ...), kind=kOutput, calls=%fused_computation.2.clone.1 | convolution fusion | flops 6467616256 | bytes 13409280 | tf_op jit(solution)/shard_map/while/body/eval_jaxpr/dot_general | solution.py:20
  192.5 12.7 %select_reduce_fusion.4 = f32[512]{0:T(512)S(1)} fusion(bf16[8192,768]{1,0:T(8,128)(2,1)} %get-tuple-element.151, s32[512]{0:T(512)S(1)} %bitcast.44, s32[8192]{0:T(1024)S(1)} %get-tuple-element.148, s32[512]{0:T(512)S(1)} %bitcast.42, pred[512]{0:T(512)(128)(4,1)S(1)} %broadcast_compare_fusion.2, bf16[4,512,768]{2,1,0:T(8,128)(2,1)} %get-tuple-element.150, ...), kind=kOutput, calls=%fused_computation.2.clone.1 | convolution fusion | flops 6467616256 | bytes 13409280 | tf_op jit(solution)/shard_map/while/body/eval_jaxpr/dot_general | solution.py:20
  205.3 12.7 %select_reduce_fusion.4 = f32[512]{0:T(512)S(1)} fusion(bf16[8192,768]{1,0:T(8,128)(2,1)} %get-tuple-element.151, s32[512]{0:T(512)S(1)} %bitcast.44, s32[8192]{0:T(1024)S(1)} %get-tuple-element.148, s32[512]{0:T(512)S(1)} %bitcast.42, pred[512]{0:T(512)(128)(4,1)S(1)} %broadcast_compare_fusion.2, bf16[4,512,768]{2,1,0:T(8,128)(2,1)} %get-tuple-element.150, ...), kind=kOutput, calls=%fused_computation.2.clone.1 | convolution fusion | flops 6467616256 | bytes 13409280 | tf_op jit(solution)/shard_map/while/body/eval_jaxpr/dot_general | solution.py:20
  218.2 12.7 %select_reduce_fusion.4 = f32[512]{0:T(512)S(1)} fusion(bf16[8192,768]{1,0:T(8,128)(2,1)} %get-tuple-element.151, s32[512]{0:T(512)S(1)} %bitcast.44, s32[8192]{0:T(1024)S(1)} %get-tuple-element.148, s32[512]{0:T(512)S(1)} %bitcast.42, pred[512]{0:T(512)(128)(4,1)S(1)} %broadcast_compare_fusion.2, bf16[4,512,768]{2,1,0:T(8,128)(2,1)} %get-tuple-element.150, ...), kind=kOutput, calls=%fused_computation.2.clone.1 | convolution fusion | flops 6467616256 | bytes 13409280 | tf_op jit(solution)/shard_map/while/body/eval_jaxpr/dot_general | solution.py:20
  231.1 14.2 %all_to_all.21 = f32[32,1,64]{2,1,0:T(1,128)S(1)} all-to-all(f32[32,1,64]{2,1,0:T(1,128)S(1)} %max_broadcast_in_dim.15), channel_id=1, replica_groups=mesh['groups'=32,'block'=4] {'groups'}, dimensions={0} | all-to-all | bytes 16384 | tf_op jit(solution)/shard_map/all_to_all | solution.py:77
  245.3 0.5 broadcast.76
  245.8 0.7 reduce.11
  246.6 1.1 select_reduce_fusion.1
  (29 shorter events, 1.0 us)
Async XLA Ops:
  6.5 173.1 %all-gather.2.cloned.1.call-start = ((), (), s32[]{:S(2)}) async-start(), calls=%async_computation.3 | async-start | bytes 15728640 | tf_op jit(solution)/shard_map/all_gather | solution.py:70
  14.7 47.2 %copy-start = (s32[512]{0:T(512)S(1)}, s32[512]{0:T(512)}, u32[]{:S(2)}) copy-start(s32[512]{0:T(512)} %param.5) | copy-start | bytes 6148
  63.2 11.1 %all-to-all-start = ((s32[32,1,64]{2,1,0:T(1,128)}), s32[32,1,64]{2,1,0:T(1,128)S(1)}, u32[]{:S(2)}, u32[]{:S(2)}) async-start(s32[32,1,64]{2,1,0:T(1,128)} %all_to_all.13), calls=%async_computation | async-start | bytes 32768 | tf_op jit(solution)/shard_map/all_to_all | solution.py:63
Sparse Core Ops, SparseCore 0:
  62.0 117.5 all-gather.1
where the time goes:
time: 256 us; the launch traced here: 255 us
  waiting for transfers between devices  98.1 us (38%)
  blocking collectives  74.5 us (29%)
  matrix products  54.1 us (21%)
  between operations  13.5 us (5%)
  other arithmetic  7.95 us (3%)
  starting transfers between devices  3.8 us (1%)
    all_gather x1, waiting for transfers between devices, body(): piece_rows = lax.all_gather(received, 'block', axis=0, tiled=True)  90.7 us
    dot_general x4, matrix products, left_turn(): lax.dot_general(part_rows, right_rows, (((1,), (1,)), ((), ())), preferre...  51 us
    all_to_all x1, blocking collectives, body(): lax.all_to_all(outgoing, 'groups', split_axis=0, concat_axis=0, tiled=True)  47.1 us
    all_to_all x1, blocking collectives, body(): lax.all_to_all(best.reshape(groups, capacity), 'groups', split_axis=0, co...  14.2 us
    all_gather x1, blocking collectives, body(): piece_ids = lax.all_gather(received_ids, 'block', axis=0, tiled=True)  13.2 us
    all_to_all x1, waiting for transfers between devices, body(): lax.all_to_all(outgoing_ids, 'groups', split_axis=0, concat_axis=0, tiled...  7.31 us
  transfers between devices with their start and end apart: 2, of which 2 were waited for; matrix products, arithmetic and copies ran while one was open for 1% of the time, Pallas kernels for 0%

commit v1 on v0

v1 whole, which is shorter than its diff:
```python
import functools
from typing import NamedTuple

import jax
import jax.numpy as jnp
import numpy as np
from jax import lax
from jax.experimental import pallas as pl
from jax.experimental.pallas import tpu as pltpu
from jax.sharding import Mesh
from jax.sharding import PartitionSpec as P

CL_GRP = 16
GROUPS = 32
GROUP_CAP = 64
WIDTH = 768
ROWS = 512
CHIPS = 64
KINDS = 4
TAIL = 16
FEATURES = 128
WIDE = WIDTH + FEATURES
LANES = 128
ALIGN = 16
COLS = 256
SAME = 4.0
HEAVY_LOAD = 72

F32 = jnp.float32
BF16 = jnp.bfloat16
I32 = jnp.int32


class Plan(NamedTuple):
    slots: int
    shift: tuple
    chunk: int
    capacity: int
    step: int
    sized: bool

    @property
    def held(self):
        return CHIPS * self.slots

    def reach(self, row):
        return row // (self.chunk // self.slots * (self.slots - 1)) * self.chunk

    def block_of(self, lane):
        return (lane * self.shift[0]) >> self.shift[1]

    def slot_of(self, lane):
        return lane - self.slots * self.block_of(lane)

    def first_lane(self):
        return self.slots * (lax.axis_index("yx") * 4 + lax.axis_index("z"))


TIGHT = Plan(24, (2731, 16), 384, 768, 384, True)
ROOMY = Plan(32, (1, 5), 256, 1280, 320, False)


def iota(shape, dim):
    return lax.broadcasted_iota(I32, shape, dim)


def deal(plan, group_hit):
    count = jnp.sum(group_hit, axis=1, keepdims=True)
    count_row = lax.dot_general(
        jnp.ones((8, ROWS), BF16),
        group_hit.astype(BF16),
        (((1,), (1,)), ((), ())),
        preferred_element_type=F32,
    )[:1]
    index = iota((GROUPS, 1), 0)
    index_row = iota((1, GROUPS), 1)
    full = (count == GROUP_CAP).astype(F32)
    heavy = jnp.sum(full * index.astype(F32), axis=0, keepdims=True).astype(I32)
    unsure = jnp.sum(full, axis=0, keepdims=True) != 1.0
    top = jnp.max(jnp.where(index == heavy, 0.0, count), axis=0, keepdims=True)

    def size_class(sizes, where):
        if plan.sized:
            value = (
                (10 * sizes > 7 * top).astype(I32)
                + (20 * sizes > 7 * top).astype(I32)
                + (50 * sizes > 9 * top).astype(I32)
            )
        else:
            value = jnp.zeros(sizes.shape, I32)
        return jnp.where(where == heavy, -1, value)

    mine = size_class(count, index)
    theirs = size_class(count_row, index_row)
    ahead = (theirs > mine) | ((theirs == mine) & (index_row < index))
    order = jnp.sum(ahead.astype(F32), axis=1, keepdims=True).astype(I32)
    ends = [jnp.sum((mine >= least).astype(F32)).astype(I32) for least in (3, 2, 1)]
    loads = [jnp.int32(0), jnp.int32(0), jnp.int32(0), jnp.int32(HEAVY_LOAD)]
    taken = [jnp.int32(0), jnp.int32(0), jnp.int32(0), jnp.int32(1)]
    code = jnp.full((GROUPS, 1), 3 * 32, I32)
    for turn in range(GROUPS - 1):
        if plan.sized:
            weight = jnp.where(
                turn < ends[0], 32, jnp.where(turn < ends[1], 16, jnp.where(turn < ends[2], 8, 4))
            )
        else:
            weight = jnp.int32(14)
        least, kind = loads[0], jnp.int32(0)
        place = taken[0]
        for other in range(1, KINDS):
            better = loads[other] < least
            least = jnp.where(better, loads[other], least)
            kind = jnp.where(better, other, kind)
            place = jnp.where(better, taken[other], place)
        for other in range(KINDS):
            chosen = kind == other
            loads[other] = loads[other] + jnp.where(chosen, weight, 0)
            taken[other] = taken[other] + jnp.where(chosen, 1, 0)
        code = jnp.where(order == turn, kind * 32 + place, code)
    return code, unsure


def send_kernel(plan, ids_ref, rows_ref, out_ref, where_ref, my_ids, my_rows, arrived):
    fetch_ids = pltpu.make_async_copy(ids_ref, my_ids, arrived.at[0])
    fetch_rows = pltpu.make_async_copy(rows_ref, my_rows, arrived.at[1])
    fetch_ids.start()
    fetch_rows.start()
    fetch_ids.wait()
    ids = my_ids[...]
    inner = ids & 15
    hit = iota((GROUPS, ROWS), 0) == (ids >> 4)
    code_of_group, unsure = deal(plan, hit.astype(F32))
    code_of_group = code_of_group.astype(F32)
    code = jnp.sum(jnp.where(hit, code_of_group, 0.0), axis=0, keepdims=True).astype(I32)
    kind, place = code >> 5, code & 31
    odd = (place & 1) == 1
    turned_in_last = (place > 0) & ((place < 4) | odd)
    turned_elsewhere = ((place + 1) & 2) == 2
    in_last = kind == KINDS - 1
    turned = (in_last & turned_in_last) | (~in_last & turned_elsewhere)
    chip = kind * 16 + jnp.where(turned, 15 - inner, inner)

    to_chip = (iota((CHIPS, ROWS), 0) == chip).astype(F32)
    earlier = (iota((ROWS, ROWS), 0) < iota((ROWS, ROWS), 1)).astype(BF16)
    rank = jnp.dot(to_chip.astype(BF16), earlier, preferred_element_type=F32)
    slot = jnp.sum(to_chip * rank, axis=0, keepdims=True).astype(I32)
    over = slot >= plan.slots - 1
    flat = jnp.where(over, -1, chip * plan.slots + slot)
    lane = jnp.where(over, -1, (plan.first_lane() + slot) & (LANES - 1))
    where_ref[...] = jnp.concatenate([chip, lane, jnp.zeros((6, ROWS), I32)], axis=0)
    lost = jnp.max(over.astype(F32), axis=1, keepdims=True)
    flag = jnp.maximum(lost, unsure.astype(F32))

    fetch_rows.wait()
    wide = my_rows[...].astype(F32)
    scale = lax.rsqrt(jnp.sum(wide * wide, axis=1, keepdims=True) + 1e-6)
    normed = (wide * scale).astype(BF16)

    at_lane = (iota((LANES, ROWS), 0) == lane).astype(BF16)
    tagged = (to_chip * (place + 1).astype(F32)).astype(BF16)
    tags = lax.dot_general(tagged, at_lane, (((1,), (1,)), ((), ())), preferred_element_type=F32)
    shown = iota((GROUPS, 128), 1) == iota((GROUPS, 128), 0) + 32
    note = jnp.sum(jnp.where(shown, code_of_group, 0.0), axis=0, keepdims=True)
    note = jnp.where(iota((1, 128), 1) == 0, flag, note)
    meta = jnp.concatenate([tags, jnp.broadcast_to(note, (CHIPS, LANES))], axis=1)
    blocks = plan.chunk // plan.slots
    for first in range(0, plan.held, plan.chunk):
        row = iota((plan.chunk, ROWS), 0) + first
        out = jnp.dot((row == flat).astype(BF16), normed, preferred_element_type=F32)
        noted = []
        for block in range(blocks):
            end = (block + 1) * plan.slots
            chip_meta = meta[first // plan.slots + block, :][None, :]
            last = jnp.where(iota((8, 2 * LANES), 0) == 7, chip_meta, 0.0)
            noted.append(out[end - plan.slots : end - 8, : 2 * LANES])
            noted.append(out[end - 8 : end, : 2 * LANES] + last)
        noted = jnp.concatenate(noted, axis=0)
        out = jnp.concatenate([noted, out[:, 2 * LANES :]], axis=1)
        out_ref[pl.ds(first, plan.chunk), :] = out.astype(BF16)


def compact_kernel(plan, held_ref, out_ref, pos_ref, total_ref):
    held = plan.held
    rows = []
    for source in range(CHIPS):
        at = (source + 1) * plan.slots - 1
        tile = held_ref[pl.ds(at // 16 * 16, 16), : 2 * LANES].astype(F32)
        rows.append(tile[at % 16 : at % 16 + 1])
    meta = jnp.concatenate(rows, axis=0)
    tags = meta[:, :LANES]
    note_top = jnp.max(meta[:, LANES:], axis=0, keepdims=True)
    note_low = jnp.min(meta[:, LANES:], axis=0, keepdims=True)
    note_lane = iota((1, 128), 1)
    flag = jnp.max(
        jnp.where(note_lane == 0, note_top, jnp.where(note_lane >= 32, note_top - note_low, 0.0))
    )
    count = jnp.sum((tags > 0).astype(F32), axis=1, keepdims=True)
    before = (iota((CHIPS, CHIPS), 1) < iota((CHIPS, CHIPS), 0)).astype(BF16)
    offset = jnp.dot(
        before, jnp.broadcast_to(count, (CHIPS, 128)).astype(BF16), preferred_element_type=F32
    )[:, :1]
    own_block = plan.block_of(iota((CHIPS, held), 1)) == iota((CHIPS, held), 0)
    tag_row = jnp.sum(
        jnp.where(own_block, jnp.concatenate([tags] * (held // LANES), axis=1), 0.0),
        axis=0,
        keepdims=True,
    )
    offset_row = jnp.sum(jnp.where(own_block, offset, 0.0), axis=0, keepdims=True).astype(I32)
    pos = jnp.where(tag_row > 0, offset_row + plan.slot_of(iota((1, held), 1)), -1)
    pos_ref[...] = jnp.broadcast_to(pos, (8, held))
    total = jnp.sum(count).astype(I32)
    source = iota((CHIPS, 1), 0)
    total_ref[pl.ds(0, ALIGN), :] = jnp.zeros((ALIGN, WIDE), BF16)
    base = 0
    chunk = plan.chunk
    for first in range(0, held, chunk):
        if first:
            low = jnp.sum(jnp.where(source == first // plan.slots, offset, 0.0)).astype(I32)
            base = pl.multiple_of((low >> 4) << 4, ALIGN)
        lanes = slice(first, first + chunk)
        take = (iota((chunk + ALIGN, chunk), 0) + base) == pos[:, lanes]
        part = jnp.dot(take.astype(BF16), held_ref[lanes, :], preferred_element_type=F32)
        tag = jnp.sum(jnp.where(take, tag_row[:, lanes], 0.0), axis=1, keepdims=True).astype(I32)
        feature = jnp.where(iota((chunk + ALIGN, FEATURES), 1) == tag - 1, 2.0, 0.0)
        part = part.astype(BF16)
        feature = feature.astype(BF16)
        head, rest = pl.ds(base, ALIGN), pl.ds(base + ALIGN, chunk)
        total_ref[head, :WIDTH] += part[:ALIGN]
        total_ref[rest, :WIDTH] = part[ALIGN:]
        total_ref[head, WIDTH:] += feature[:ALIGN]
        total_ref[rest, WIDTH:] = feature[ALIGN:]

    def clear(tile, carry):
        rows = pl.ds(pl.multiple_of(tile * ALIGN, ALIGN), ALIGN)
        total_ref[rows, :] = jnp.zeros((ALIGN, WIDE), BF16)
        return carry

    lax.fori_loop((base + chunk + ALIGN) >> 4, plan.capacity // ALIGN, clear, 0)
    out_ref[pl.ds(0, plan.capacity), :] = total_ref[pl.ds(0, plan.capacity), :]
    flag = jnp.maximum(flag, (total > plan.capacity).astype(F32))
    note = jnp.where(note_lane == 0, flag, jnp.where(note_lane >= 32, note_top, 0.0))
    tail = jnp.concatenate([note, jnp.zeros((1, WIDE - 128), F32)], axis=1)
    out_ref[pl.ds(plan.capacity, TAIL), :] = jnp.broadcast_to(tail, (TAIL, WIDE)).astype(BF16)


def score_block(plan, own_ref, rows_ref, start, best, same):
    own = own_ref[pl.ds(start, COLS), :]
    for first in range(0, plan.capacity, plan.step):
        rows = rows_ref[pl.ds(first, plan.step), :]
        scores = lax.dot_general(
            rows, own, (((1,), (1,)), ((), ())), preferred_element_type=F32
        )
        if same:
            row_index = iota((plan.step, COLS), 0) + first
            scores = jnp.where(row_index == iota((plan.step, COLS), 1) + start, -1.0, scores)
        best = jnp.maximum(best, jnp.max(scores.reshape(plan.step // 8, 8, COLS), axis=0))
    return best


def own_kernel(plan, own_ref, out_ref):
    for start in range(0, plan.capacity, COLS):
        best = jnp.full((8, COLS), -1.0, F32)
        out_ref[:, pl.ds(start, COLS)] = score_block(plan, own_ref, own_ref, start, best, True)


def other_kernel(
    plan, pos_ref, own_ref, other_ref, part_ref, out_ref
):
    own_note = own_ref[pl.ds(plan.capacity, TAIL), :128].astype(F32)
    other_note = other_ref[pl.ds(plan.capacity, TAIL), :128].astype(F32)
    note_lane = iota((TAIL, 128), 1)
    differs = (note_lane >= 32) & (own_note != other_note)
    raised = jnp.where(note_lane == 0, jnp.maximum(own_note, other_note), 0.0)
    flag = jnp.max(jnp.where(differs, 1.0, raised))
    found = [jnp.zeros((8, plan.chunk), F32)] * (plan.held // plan.chunk)
    for start in range(0, plan.capacity, COLS):
        best = score_block(plan, own_ref, other_ref, start, part_ref[:, pl.ds(start, COLS)], False)
        top = jnp.max(jnp.transpose(best), axis=1, keepdims=True) - SAME
        top = jnp.maximum(top, -1.0)
        row = iota((COLS, plan.chunk), 0) + start
        for index in range(plan.reach(start) // plan.chunk, plan.held // plan.chunk):
            pos = pos_ref[0:1, index * plan.chunk : (index + 1) * plan.chunk]
            value = jnp.where(row == pos, top, 0.0)
            found[index] += jnp.sum(value.reshape(COLS // 8, 8, plan.chunk), axis=0)

    blocks = plan.chunk // plan.slots
    for index, values in enumerate(found):
        lane = iota((1, plan.chunk), 1)
        values = jnp.sum(values, axis=0, keepdims=True)
        values = jnp.where(plan.slot_of(lane) == plan.slots - 1, flag, values)
        in_block = plan.block_of(lane) == iota((blocks, plan.chunk), 0)
        mine = jnp.where(in_block, values, 0.0)
        folded = mine[:, :LANES]
        for first in range(LANES, plan.chunk, LANES):
            folded = folded + mine[:, first : first + LANES]
        out_ref[index * blocks : (index + 1) * blocks, :] = folded


def answer_kernel(plan, where_ref, back_ref, out_ref, flag_ref):
    chip = where_ref[0:1, :]
    lane = where_ref[1:2, :]
    back = back_ref[...]
    to_chip = (iota((CHIPS, ROWS), 0) == chip).astype(F32)
    by_row = lax.dot_general(
        back,
        to_chip,
        (((0,), (0,)), ((), ())),
        preferred_element_type=F32,
        precision=lax.Precision.HIGHEST,
    )
    at_lane = iota((LANES, ROWS), 0) == lane
    out_ref[...] = jnp.sum(jnp.where(at_lane, by_row, 0.0), axis=0, keepdims=True)
    last = iota((CHIPS, LANES), 1) == ((plan.first_lane() + plan.slots - 1) & (LANES - 1))
    flag_ref[0] = (jnp.max(jnp.where(last, back, 0.0)) > 0.0).astype(I32)


VMEM = pl.BlockSpec(memory_space=pltpu.VMEM)
SMEM = pl.BlockSpec(memory_space=pltpu.SMEM)
HBM = pl.BlockSpec(memory_space=pltpu.HBM)


def shape(dims, dtype):
    return jax.ShapeDtypeStruct(dims, dtype)


def call(kernel, plan, name, **options):
    return pl.pallas_call(
        functools.partial(kernel, plan),
        compiler_params=pltpu.CompilerParams(vmem_limit_bytes=48 * 1024 * 1024),
        name=name,
        **options,
    )


def swap(plan, message):
    return lax.all_to_all(message, ("yx", "z"), split_axis=0, concat_axis=0, tiled=True)


def owner_path(plan, embeddings, cluster_ids):
    message, where = call(
        send_kernel,
        plan,
        "send",
        out_shape=(shape((plan.held, WIDTH), BF16), shape((8, ROWS), I32)),
        in_specs=[HBM, HBM],
        out_specs=(VMEM, VMEM),
        scratch_shapes=[
            pltpu.VMEM((1, ROWS), I32),
            pltpu.VMEM((ROWS, WIDTH), BF16),
            pltpu.SemaphoreType.DMA((2,)),
        ],
    )(cluster_ids.reshape(1, ROWS), embeddings)
    held = swap(plan, message)
    packed, pos = call(
        compact_kernel,
        plan,
        "compact",
        out_shape=(
            shape((plan.capacity + TAIL, WIDE), BF16),
            shape((8, plan.held), I32),
        ),
        in_specs=[VMEM],
        out_specs=(VMEM, VMEM),
        scratch_shapes=[pltpu.VMEM((plan.held + plan.chunk + ALIGN, WIDE), BF16)],
    )(held)
    other = lax.ppermute(packed, "core", [(0, 1), (1, 0)])
    part = call(
        own_kernel,
        plan,
        "score_own",
        out_shape=shape((8, plan.capacity), F32),
        in_specs=[VMEM],
        out_specs=VMEM,
        cost_estimate=pl.CostEstimate(
            flops=2 * plan.capacity**2 * WIDE,
            bytes_accessed=2 * plan.capacity * WIDE,
            transcendentals=0,
        ),
    )(packed)
    best = call(
        other_kernel,
        plan,
        "score_other",
        out_shape=shape((CHIPS, LANES), F32),
        in_specs=[VMEM, VMEM, VMEM, VMEM],
        out_specs=VMEM,
    )(pos, packed, other, part)
    back = swap(plan, best)
    answer, flag = call(
        answer_kernel,
        plan,
        "answer",
        out_shape=(shape((1, ROWS), F32), shape((1,), I32)),
        in_specs=[VMEM, VMEM],
        out_specs=(VMEM, SMEM),
    )(where, back)
    return answer.reshape(ROWS), flag[0]


def pair_max(left_rows, left_ids, left_pos, right_rows, right_ids, right_pos):
    left_total, width = left_rows.shape
    left_step = min(512, left_total)
    left_count = left_total // left_step

    def left_turn(carry, left_tuple):
        part_rows, part_ids, part_pos = left_tuple
        scores = lax.dot_general(
            part_rows, right_rows, (((1,), (1,)), ((), ())), preferred_element_type=F32
        )
        matches = (
            (part_ids[:, None] == right_ids[None, :])
            & (part_ids[:, None] >= 0)
            & (part_pos[:, None] != right_pos[None, :])
        )
        return carry, jnp.max(jnp.where(matches, scores, -1.0), axis=1)

    _, row_best = lax.scan(
        left_turn,
        0,
        (
            left_rows.reshape(left_count, left_step, width),
            left_ids.reshape(left_count, left_step),
            left_pos.reshape(left_count, left_step),
        ),
    )
    return row_best.reshape(-1)


def gather(piece):
    copies = jnp.broadcast_to(piece[None], (4, *piece.shape))
    whole = lax.all_to_all(copies, "z", split_axis=0, concat_axis=0, tiled=True)
    return whole.reshape(-1, *piece.shape[1:])


def any_path(embeddings, cluster_ids):
    axes = ("yx", "core")
    widened = embeddings.astype(F32)
    normed = (
        widened * lax.rsqrt(jnp.sum(widened * widened, axis=1, keepdims=True) + 1e-06)
    ).astype(BF16)
    owner_group = cluster_ids // CL_GRP
    one_hot = (owner_group[:, None] == jnp.arange(GROUPS, dtype=I32)[None, :]).astype(I32)
    slot_index = jnp.sum(jnp.cumsum(one_hot, axis=0) * one_hot, axis=1) - 1
    flat_slot = owner_group * GROUP_CAP + slot_index
    total = GROUPS * GROUP_CAP
    placement = jnp.arange(total, dtype=I32)[:, None] == flat_slot[None, :]
    outgoing = jnp.dot(placement.astype(BF16), normed, preferred_element_type=F32).astype(BF16)
    outgoing = outgoing.reshape(GROUPS, GROUP_CAP, WIDTH)
    outgoing_ids = jnp.max(jnp.where(placement, cluster_ids[None, :], -1), axis=1)
    outgoing_ids = outgoing_ids.reshape(GROUPS, GROUP_CAP)
    received = lax.all_to_all(outgoing, axes, 0, 0, tiled=True).reshape(total, WIDTH)
    received_ids = lax.all_to_all(outgoing_ids, axes, 0, 0, tiled=True).reshape(total)
    own_pos = jnp.arange(total, dtype=I32) + lax.axis_index("z") * total
    piece_rows = gather(received)
    piece_ids = gather(received_ids)
    piece_pos = jnp.arange(piece_rows.shape[0], dtype=I32)
    best = pair_max(received, received_ids, own_pos, piece_rows, piece_ids, piece_pos)
    best = jnp.maximum(best, -1.0)
    returned = lax.all_to_all(best.reshape(GROUPS, GROUP_CAP), axes, 0, 0, tiled=True)
    return jnp.max(jnp.where(placement, returned.reshape(total)[:, None], -2.0), axis=0)


def body(embeddings, cluster_ids):
    def keep(rows, ids, done):
        return done

    def last_resort(rows, ids, done):
        return any_path(rows, ids)

    def roomy(rows, ids, done):
        answer, flag = owner_path(ROOMY, rows, ids)
        return lax.switch(flag, [keep, last_resort], rows, ids, answer)

    answer, flag = owner_path(TIGHT, embeddings, cluster_ids)
    return lax.switch(flag, [keep, roomy], embeddings, cluster_ids, answer)


def solution(mesh):
    chips = Mesh(np.asarray(mesh.devices).reshape(16, 2, 4), ("yx", "core", "z"))
    axes = ("yx", "core", "z")
    return jax.shard_map(
        body, mesh=chips, in_specs=(P(axes, None), P(axes)), out_specs=P(axes), check_vma=False
    )
```

time: 256 us -> 72.5 us (0.28)
  waiting for transfers between devices: 98.1 us -> 11.3 us
  matrix products: 54.1 us -> 0 us
  blocking collectives: 74.5 us -> 44.3 us
  between operations: 13.5 us -> 0.94 us
  Pallas kernels: 0 us -> 10.4 us
  other arithmetic: 7.95 us -> 0 us
    all_gather x1 -> x0, waiting for transfers between devices: 90.7 us -> none  [body(): piece_rows = lax.all_gather(received, 'block', axis=0, tiled=True)]
    dot_general x5 -> x0, matrix products: 54.1 us -> none  [the longest x4 51 us: left_turn(): lax.dot_general(part_rows, right_rows, (((1,), (1,)), ((), ())), preferre...]
    all_to_all x2 -> x1, blocking collectives: 61.3 us -> 44.3 us  [swap(): lax.all_to_all(message, ('yx', 'z'), split_axis=0, concat_axis=0, tiled=T...]
    all_gather x1 -> x0, blocking collectives: 13.2 us -> none  [body(): piece_ids = lax.all_gather(received_ids, 'block', axis=0, tiled=True)]
    pallas_call x0 -> x5, Pallas kernels: none -> 10.4 us  [the longest x1 3.27 us: owner_path(): call(send_kernel, plan, 'send', out_shape=(shape((plan.held, WIDTH), BF16...]
  transfers between devices with their start and end apart: 2 -> 2, of which waited for: 2 -> 2; matrix products, arithmetic and copies ran while one was open for 1% -> 0% of each run, Pallas kernels for 0% -> 2%
where the time goes in v1:
time: 72.5 us; the launch traced here: 72.3 us
  blocking collectives  44.3 us (61%)
  waiting for transfers between devices  11.3 us (16%)
  Pallas kernels  10.4 us (14%)
  starting transfers between devices  5.14 us (7%)
  between operations  0.94 us (1%)
    all_to_all x1, blocking collectives, swap(): lax.all_to_all(message, ('yx', 'z'), split_axis=0, concat_axis=0, tiled=T...  44.3 us
    all_to_all x1, waiting for transfers between devices, swap(): lax.all_to_all(message, ('yx', 'z'), split_axis=0, concat_axis=0, tiled=T...  9.54 us
    all_to_all x1, starting transfers between devices, swap(): lax.all_to_all(message, ('yx', 'z'), split_axis=0, concat_axis=0, tiled=T...  5.05 us
    pallas_call x1, Pallas kernels, owner_path(): call(send_kernel, plan, 'send', out_shape=(shape((plan.held, WIDTH), BF16...  3.27 us
    pallas_call x1, Pallas kernels, owner_path(): call(other_kernel, plan, 'score_other', out_shape=shape((CHIPS, LANES), F...  2.46 us
    pallas_call x1, Pallas kernels, owner_path(): call(compact_kernel, plan, 'compact', out_shape=(shape((plan.capacity + T...  2.21 us
    ppermute x1, waiting for transfers between devices, owner_path(): other = lax.ppermute(packed, 'core', [(0, 1), (1, 0)])  1.74 us
  transfers between devices with their start and end apart: 2, of which 2 were waited for; matrix products, arithmetic and copies ran while one was open for 0% of the time, Pallas kernels for 2%

profile of v1, /device:TPU:0, one launch (start us, length us, event | category | flops | bytes accessed | tf_op | source)
XLA Modules:
  0.0 72.3 jit_solution(13994877852788766730)
XLA Ops:
  0.0 3.3 %send.3 = (bf16[1536,768]{1,0:T(8,128)(2,1)S(1)}, s32[8,512]{1,0:T(8,128)S(1)}) custom-call(s32[1,512]{1,0:T(1,128)} %bitcast.82, bf16[512,768]{1,0:T(8,128)(2,1)} %rows_ref.1), custom_call_target="tpu_custom_call" | custom-call | tf_op jit(solution)/shard_map/send/pallas_call | solution.py:340
  3.3 44.3 %all_to_all.69 = bf16[64,24,768]{2,1,0:T(8,128)(2,1)S(1)} all-to-all(bf16[64,24,768]{2,1,0:T(8,128)(2,1)S(1)} %bitcast.69), channel_id=1, replica_groups=mesh['yx'=16,'core'=2,'z'=4] {'yx','z'}, dimensions={0} | all-to-all | bytes 4718592 | tf_op jit(solution)/shard_map/all_to_all | solution.py:336
  47.6 0.0 copy-start
  47.6 0.0 copy-start.1
  47.6 2.2 %compact.3 = (bf16[784,896]{1,0:T(8,128)(2,1)S(1)}, s32[8,1536]{1,0:T(8,128)S(1)}) custom-call(bf16[1536,768]{1,0:T(8,128)(2,1)S(1)} %bitcast.67), custom_call_target="tpu_custom_call" | custom-call | tf_op jit(solution)/shard_map/compact/pallas_call | solution.py:354
  49.8 0.1 collective-permute-start.1
  49.9 1.4 %score_own.3.part_ref = f32[8,768]{1,0:T(8,128)S(1)} custom-call(bf16[784,896]{1,0:T(8,128)(2,1)S(1)} %get-tuple-element.86.own_ref), custom_call_target="tpu_custom_call" | custom-call | flops 1056964608 | bytes 1376256 | tf_op jit(solution)/shard_map/score_own/pallas_call | solution.py:367
  51.3 1.7 %collective-permute-done.1.other_ref = bf16[784,896]{1,0:T(8,128)(2,1)S(1)} collective-permute-done((bf16[784,896]{1,0:T(8,128)(2,1)S(1)}, bf16[784,896]{1,0:T(8,128)(2,1)S(1)}, u32[]{:S(2)}, u32[]{:S(2)}) %collective-permute-start.1) | collective-permute-done | bytes 1404960 | tf_op jit(solution)/shard_map/ppermute | solution.py:366
  53.1 2.5 %score_other.3 = f32[64,128]{1,0:T(8,128)} custom-call(s32[8,1536]{1,0:T(8,128)S(1)} %get-tuple-element.85.pos_ref, bf16[784,896]{1,0:T(8,128)(2,1)S(1)} %get-tuple-element.86.own_ref, bf16[784,896]{1,0:T(8,128)(2,1)S(1)} %collective-permute-done.1.other_ref, f32[8,768]{1,0:T(8,128)S(1)} %score_own.3.part_ref), custom_call_target="tpu_custom_call" | custom-call | tf_op jit(solution)/shard_map/score_other/pallas_call | solution.py:380
  55.5 5.1 %all-to-all-start.8 = ((f32[64,1,128]{2,1,0:T(1,128)}), f32[64,1,128]{2,1,0:T(1,128)S(1)}, u32[]{:S(2)}, u32[]{:S(2)}) async-start(f32[64,1,128]{2,1,0:T(1,128)} %bitcast.19), calls=%async_computation.8 | async-start | bytes 65536 | tf_op jit(solution)/shard_map/all_to_all | solution.py:336
  60.6 9.5 %all-to-all-done.8 = f32[64,1,128]{2,1,0:T(1,128)S(1)} async-done(((f32[64,1,128]{2,1,0:T(1,128)}), f32[64,1,128]{2,1,0:T(1,128)S(1)}, u32[]{:S(2)}, u32[]{:S(2)}) %all-to-all-start.8) | async-done | bytes 32800 | tf_op jit(solution)/shard_map/all_to_all | solution.py:336
  70.1 1.0 %answer.3 = (f32[1,512]{1,0:T(1,128)}, s32[1]{0:T(128)}) custom-call(s32[8,512]{1,0:T(8,128)S(1)} %get-tuple-element.83.where_ref, f32[64,128]{1,0:T(8,128)S(1)} %bitcast.71), custom_call_target="tpu_custom_call" | custom-call | tf_op jit(solution)/shard_map/answer/pallas_call | solution.py:389
  71.8 0.0 copy-done
  71.9 0.0 copy-done.1
  71.9 0.2 conditional.2
Async XLA Ops:
  47.6 24.2 %copy-start = (bf16[512,768]{1,0:T(8,128)(2,1)S(1)}, bf16[512,768]{1,0:T(8,128)(2,1)}, u32[]{:S(2)}) copy-start(bf16[512,768]{1,0:T(8,128)(2,1)} %rows_ref.1) | copy-start | bytes 2359300
  47.6 24.3 %copy-start.1 = (s32[512]{0:T(512)S(1)}, s32[512]{0:T(512)}, u32[]{:S(2)}) copy-start(s32[512]{0:T(512)} %param.9) | copy-start | bytes 6148
  49.8 3.2 %collective-permute-start.1 = (bf16[784,896]{1,0:T(8,128)(2,1)S(1)}, bf16[784,896]{1,0:T(8,128)(2,1)S(1)}, u32[]{:S(2)}, u32[]{:S(2)}) collective-permute-start(bf16[784,896]{1,0:T(8,128)(2,1)S(1)} %get-tuple-element.86.own_ref), channel_id=1, source_target_pairs={{0,4},{4,0},{1,5},{5,1},{2,6},{6,2},{3,7},{7,3},{8,12},{12,8},{9,1... | collective-permute-start | bytes 4214792 | tf_op jit(solution)/shard_map/ppermute | solution.py:366
  55.5 14.6 %all-to-all-start.8 = ((f32[64,1,128]{2,1,0:T(1,128)}), f32[64,1,128]{2,1,0:T(1,128)S(1)}, u32[]{:S(2)}, u32[]{:S(2)}) async-start(f32[64,1,128]{2,1,0:T(1,128)} %bitcast.19), calls=%async_computation.8 | async-start | bytes 65536 | tf_op jit(solution)/shard_map/all_to_all | solution.py:336

commit v2 on v1

--- a/solution.py
+++ b/solution.py
@@ -18,12 +18,9 @@
 CHIPS = 64
 KINDS = 4
 TAIL = 16
-FEATURES = 128
-WIDE = WIDTH + FEATURES
 LANES = 128
 ALIGN = 16
 COLS = 256
-SAME = 4.0
 HEAVY_LOAD = 72
 
 F32 = jnp.float32
@@ -42,6 +39,10 @@
     @property
     def held(self):
         return CHIPS * self.slots
+
+    @property
+    def tail(self):
+        return -(-self.capacity // WIDTH) * TAIL
 
     def reach(self, row):
         return row // (self.chunk // self.slots * (self.slots - 1)) * self.chunk
@@ -179,7 +180,7 @@
         out_ref[pl.ds(first, plan.chunk), :] = out.astype(BF16)
 
 
-def compact_kernel(plan, held_ref, out_ref, pos_ref, total_ref):
+def compact_kernel(plan, held_ref, out_ref, tags_ref, pos_ref, total_ref, tag_ref):
     held = plan.held
     rows = []
     for source in range(CHIPS):
@@ -210,7 +211,8 @@
     pos_ref[...] = jnp.broadcast_to(pos, (8, held))
     total = jnp.sum(count).astype(I32)
     source = iota((CHIPS, 1), 0)
-    total_ref[pl.ds(0, ALIGN), :] = jnp.zeros((ALIGN, WIDE), BF16)
+    total_ref[pl.ds(0, ALIGN), :] = jnp.zeros((ALIGN, WIDTH), BF16)
+    tag_ref[pl.ds(0, ALIGN), :] = jnp.zeros((ALIGN, LANES), BF16)
     base = 0
     chunk = plan.chunk
     for first in range(0, held, chunk):
@@ -220,68 +222,90 @@
         lanes = slice(first, first + chunk)
         take = (iota((chunk + ALIGN, chunk), 0) + base) == pos[:, lanes]
         part = jnp.dot(take.astype(BF16), held_ref[lanes, :], preferred_element_type=F32)
-        tag = jnp.sum(jnp.where(take, tag_row[:, lanes], 0.0), axis=1, keepdims=True).astype(I32)
-        feature = jnp.where(iota((chunk + ALIGN, FEATURES), 1) == tag - 1, 2.0, 0.0)
+        tag = jnp.sum(jnp.where(take, tag_row[:, lanes], 0.0), axis=1, keepdims=True)
+        tag = jnp.broadcast_to(tag, (chunk + ALIGN, LANES)).astype(BF16)
         part = part.astype(BF16)
-        feature = feature.astype(BF16)
         head, rest = pl.ds(base, ALIGN), pl.ds(base + ALIGN, chunk)
-        total_ref[head, :WIDTH] += part[:ALIGN]
-        total_ref[rest, :WIDTH] = part[ALIGN:]
-        total_ref[head, WIDTH:] += feature[:ALIGN]
-        total_ref[rest, WIDTH:] = feature[ALIGN:]
+        total_ref[head, :] += part[:ALIGN]
+        total_ref[rest, :] = part[ALIGN:]
+        tag_ref[head, :] += tag[:ALIGN]
+        tag_ref[rest, :] = tag[ALIGN:]
 
     def clear(tile, carry):
         rows = pl.ds(pl.multiple_of(tile * ALIGN, ALIGN), ALIGN)
-        total_ref[rows, :] = jnp.zeros((ALIGN, WIDE), BF16)
+        total_ref[rows, :] = jnp.zeros((ALIGN, WIDTH), BF16)
+        tag_ref[rows, :] = jnp.zeros((ALIGN, LANES), BF16)
         return carry
 
     lax.fori_loop((base + chunk + ALIGN) >> 4, plan.capacity // ALIGN, clear, 0)
     out_ref[pl.ds(0, plan.capacity), :] = total_ref[pl.ds(0, plan.capacity), :]
+    tags = tag_ref[pl.ds(0, plan.capacity), :]
+    tags_ref[...] = tags
+    one_lane = (iota((TAIL, LANES), 1) == 0).astype(BF16)
+    tag_lanes = lax.dot_general(
+        one_lane, tags, (((1,), (1,)), ((), ())), preferred_element_type=F32
+    )
     flag = jnp.maximum(flag, (total > plan.capacity).astype(F32))
     note = jnp.where(note_lane == 0, flag, jnp.where(note_lane >= 32, note_top, 0.0))
-    tail = jnp.concatenate([note, jnp.zeros((1, WIDE - 128), F32)], axis=1)
-    out_ref[pl.ds(plan.capacity, TAIL), :] = jnp.broadcast_to(tail, (TAIL, WIDE)).astype(BF16)
-
-
-def score_block(plan, own_ref, rows_ref, start, best, same):
-    own = own_ref[pl.ds(start, COLS), :]
-    for first in range(0, plan.capacity, plan.step):
-        rows = rows_ref[pl.ds(first, plan.step), :]
+    note = jnp.concatenate([note, jnp.zeros((1, plan.capacity - LANES), F32)], axis=1)
+    tail = jnp.where(iota((TAIL, plan.capacity), 0) < TAIL // 2, note, tag_lanes)
+    for first in range(0, plan.capacity, WIDTH):
+        piece = tail[:, first : first + WIDTH].astype(BF16)
+        out_ref[pl.ds(plan.capacity + first // WIDTH * TAIL, TAIL), : piece.shape[1]] = piece
+
+
+def tail_of(plan, ref):
+    pieces = []
+    for first in range(0, plan.capacity, WIDTH):
+        rows = pl.ds(plan.capacity + first // WIDTH * TAIL, TAIL)
+        pieces.append(ref[rows, : min(WIDTH, plan.capacity - first)].astype(F32))
+    tail = jnp.concatenate(pieces, axis=1)
+    return tail[:1, :LANES], tail[TAIL // 2 : TAIL // 2 + 1, :]
+
+
+def score_block(plan, own_ref, tags_ref, rows_ref, row_tags, start, best, same):
+    own = own_ref[pl.ds(start, plan.step), :]
+    own_tag = tags_ref[pl.ds(start, plan.step), :1].astype(F32)
+    for first in range(0, plan.capacity, COLS):
+        rows = rows_ref[pl.ds(first, COLS), :]
         scores = lax.dot_general(
-            rows, own, (((1,), (1,)), ((), ())), preferred_element_type=F32
+            own, rows, (((1,), (1,)), ((), ())), preferred_element_type=F32
         )
+        match = own_tag == row_tags[:, first : first + COLS]
         if same:
-            row_index = iota((plan.step, COLS), 0) + first
-            scores = jnp.where(row_index == iota((plan.step, COLS), 1) + start, -1.0, scores)
-        best = jnp.maximum(best, jnp.max(scores.reshape(plan.step // 8, 8, COLS), axis=0))
+            index = iota((plan.step, COLS), 0) + (start - first)
+            match = match & (index != iota((plan.step, COLS), 1))
+        scores = jnp.where(match, scores, -1.0)
+        for lane in range(0, COLS, LANES):
+            best = jnp.maximum(best, scores[:, lane : lane + LANES])
     return best
 
 
-def own_kernel(plan, own_ref, out_ref):
-    for start in range(0, plan.capacity, COLS):
-        best = jnp.full((8, COLS), -1.0, F32)
-        out_ref[:, pl.ds(start, COLS)] = score_block(plan, own_ref, own_ref, start, best, True)
-
-
-def other_kernel(
-    plan, pos_ref, own_ref, other_ref, part_ref, out_ref
-):
-    own_note = own_ref[pl.ds(plan.capacity, TAIL), :128].astype(F32)
-    other_note = other_ref[pl.ds(plan.capacity, TAIL), :128].astype(F32)
-    note_lane = iota((TAIL, 128), 1)
+def own_kernel(plan, own_ref, tags_ref, out_ref):
+    _, own_tags = tail_of(plan, own_ref)
+    for start in range(0, plan.capacity, plan.step):
+        best = jnp.full((plan.step, LANES), -1.0, F32)
+        best = score_block(plan, own_ref, tags_ref, own_ref, own_tags, start, best, True)
+        out_ref[pl.ds(start, plan.step), :] = best
+
+
+def other_kernel(plan, pos_ref, own_ref, tags_ref, other_ref, part_ref, out_ref):
+    own_note, _ = tail_of(plan, own_ref)
+    other_note, other_tags = tail_of(plan, other_ref)
+    note_lane = iota((1, LANES), 1)
     differs = (note_lane >= 32) & (own_note != other_note)
     raised = jnp.where(note_lane == 0, jnp.maximum(own_note, other_note), 0.0)
-    flag = jnp.max(jnp.where(differs, 1.0, raised))
+    flag = jnp.max(jnp.where(differs, 1.0, raised), axis=1, keepdims=True)
     found = [jnp.zeros((8, plan.chunk), F32)] * (plan.held // plan.chunk)
-    for start in range(0, plan.capacity, COLS):
-        best = score_block(plan, own_ref, other_ref, start, part_ref[:, pl.ds(start, COLS)], False)
-        top = jnp.max(jnp.transpose(best), axis=1, keepdims=True) - SAME
-        top = jnp.maximum(top, -1.0)
-        row = iota((COLS, plan.chunk), 0) + start
+    for start in range(0, plan.capacity, plan.step):
+        best = part_ref[pl.ds(start, plan.step), :]
+        best = score_block(plan, own_ref, tags_ref, other_ref, other_tags, start, best, False)
+        top = jnp.max(best, axis=1, keepdims=True)
+        row = iota((plan.step, plan.chunk), 0) + start
         for index in range(plan.reach(start) // plan.chunk, plan.held // plan.chunk):
             pos = pos_ref[0:1, index * plan.chunk : (index + 1) * plan.chunk]
             value = jnp.where(row == pos, top, 0.0)
-            found[index] += jnp.sum(value.reshape(COLS // 8, 8, plan.chunk), axis=0)
+            found[index] += jnp.sum(value.reshape(plan.step // 8, 8, plan.chunk), axis=0)
 
     blocks = plan.chunk // plan.slots
     for index, values in enumerate(found):
@@ -351,40 +375,44 @@
         ],
     )(cluster_ids.reshape(1, ROWS), embeddings)
     held = swap(plan, message)
-    packed, pos = call(
+    packed, tags, pos = call(
         compact_kernel,
         plan,
         "compact",
         out_shape=(
-            shape((plan.capacity + TAIL, WIDE), BF16),
+            shape((plan.capacity + plan.tail, WIDTH), BF16),
+            shape((plan.capacity, LANES), BF16),
             shape((8, plan.held), I32),
         ),
         in_specs=[VMEM],
-        out_specs=(VMEM, VMEM),
-        scratch_shapes=[pltpu.VMEM((plan.held + plan.chunk + ALIGN, WIDE), BF16)],
+        out_specs=(VMEM, VMEM, VMEM),
+        scratch_shapes=[
+            pltpu.VMEM((plan.held + plan.chunk + ALIGN, WIDTH), BF16),
+            pltpu.VMEM((plan.held + plan.chunk + ALIGN, LANES), BF16),
+        ],
     )(held)
     other = lax.ppermute(packed, "core", [(0, 1), (1, 0)])
     part = call(
         own_kernel,
         plan,
         "score_own",
-        out_shape=shape((8, plan.capacity), F32),
-        in_specs=[VMEM],
+        out_shape=shape((plan.capacity, LANES), F32),
+        in_specs=[VMEM, VMEM],
         out_specs=VMEM,
         cost_estimate=pl.CostEstimate(
-            flops=2 * plan.capacity**2 * WIDE,
-            bytes_accessed=2 * plan.capacity * WIDE,
+            flops=2 * plan.capacity**2 * WIDTH,
+            bytes_accessed=2 * plan.capacity * WIDTH,
             transcendentals=0,
         ),
-    )(packed)
+    )(packed, tags)
     best = call(
         other_kernel,
         plan,
         "score_other",
         out_shape=shape((CHIPS, LANES), F32),
-        in_specs=[VMEM, VMEM, VMEM, VMEM],
+        in_specs=[VMEM] * 5,
         out_specs=VMEM,
-    )(pos, packed, other, part)
+    )(pos, packed, tags, other, part)
     back = swap(plan, best)
     answer, flag = call(
         answer_kernel,
@@ -472,6 +500,9 @@
         return lax.switch(flag, [keep, last_resort], rows, ids, answer)
 
     answer, flag = owner_path(TIGHT, embeddings, cluster_ids)
+    embeddings, cluster_ids, answer, flag = lax.optimization_barrier(
+        (embeddings, cluster_ids, answer, flag)
+    )
     return lax.switch(flag, [keep, roomy], embeddings, cluster_ids, answer)
 
 

time: 72.5 us -> 71.1 us (0.981)
  blocking collectives: 44.3 us -> 58.7 us
  waiting for transfers between devices: 11.3 us -> 1.74 us
  starting transfers between devices: 5.14 us -> 0.09 us
  Pallas kernels: 10.4 us -> 9.12 us
    all_to_all x1 -> x2, blocking collectives: 44.3 us -> 58.7 us  [swap(): lax.all_to_all(message, ('yx', 'z'), split_axis=0, concat_axis=0, tiled=T...]
    all_to_all x1 -> x0, waiting for transfers between devices: 9.54 us -> none  [swap(): lax.all_to_all(message, ('yx', 'z'), split_axis=0, concat_axis=0, tiled=T...]
    all_to_all x1 -> x0, starting transfers between devices: 5.05 us -> none  [swap(): lax.all_to_all(message, ('yx', 'z'), split_axis=0, concat_axis=0, tiled=T...]
    pallas_call x1, Pallas kernels: 2.46 us -> 1.5 us  [owner_path(): call(other_kernel, plan, 'score_other', out_shape=shape((CHIPS, LANES), F...]
  transfers between devices with their start and end apart: 2 -> 1, of which waited for: 2 -> 1; matrix products, arithmetic and copies ran while one was open for 0% -> 0% of each run, Pallas kernels for 2% -> 2%
where the time goes in v2:
time: 71.1 us; the launch traced here: 70.9 us
  blocking collectives  58.7 us (83%)
  Pallas kernels  9.12 us (13%)
  waiting for transfers between devices  1.74 us (2%)
  between operations  1 us (1%)
    all_to_all x2, blocking collectives, swap(): lax.all_to_all(message, ('yx', 'z'), split_axis=0, concat_axis=0, tiled=T...  58.7 us
    pallas_call x1, Pallas kernels, owner_path(): call(send_kernel, plan, 'send', out_shape=(shape((plan.held, WIDTH), BF16...  3.27 us
    pallas_call x1, Pallas kernels, owner_path(): call(compact_kernel, plan, 'compact', out_shape=(shape((plan.capacity + p...  2.22 us
    ppermute x1, waiting for transfers between devices, owner_path(): other = lax.ppermute(packed, 'core', [(0, 1), (1, 0)])  1.74 us
    pallas_call x1, Pallas kernels, owner_path(): call(other_kernel, plan, 'score_other', out_shape=shape((CHIPS, LANES), F...  1.5 us
  transfers between devices with their start and end apart: 1, of which 1 were waited for; matrix products, arithmetic and copies ran while one was open for 0% of the time, Pallas kernels for 2%

profile of v2, /device:TPU:0, one launch (start us, length us, event | category | flops | bytes accessed | tf_op | source)
XLA Modules:
  0.0 70.9 jit_solution(9207848439642412422)
XLA Ops:
  0.0 3.3 %send.3 = (bf16[1536,768]{1,0:T(8,128)(2,1)S(1)}, s32[8,512]{1,0:T(8,128)S(1)}) custom-call(s32[1,512]{1,0:T(1,128)} %bitcast.83, bf16[512,768]{1,0:T(8,128)(2,1)} %rows_ref.1), custom_call_target="tpu_custom_call" | custom-call | tf_op jit(solution)/shard_map/send/pallas_call | solution.py:364
  3.3 44.3 %all_to_all.69 = bf16[64,24,768]{2,1,0:T(8,128)(2,1)S(1)} all-to-all(bf16[64,24,768]{2,1,0:T(8,128)(2,1)S(1)} %bitcast.69), channel_id=1, replica_groups=mesh['yx'=16,'core'=2,'z'=4] {'yx','z'}, dimensions={0} | all-to-all | bytes 4718592 | tf_op jit(solution)/shard_map/all_to_all | solution.py:360
  47.6 0.0 copy-start
  47.6 0.0 copy-start.1
  47.6 2.2 %compact.3 = (bf16[784,768]{1,0:T(8,128)(2,1)S(1)}, bf16[768,128]{1,0:T(8,128)(2,1)S(1)}, s32[8,1536]{1,0:T(8,128)S(1)}) custom-call(bf16[1536,768]{1,0:T(8,128)(2,1)S(1)} %bitcast.67), custom_call_target="tpu_custom_call" | custom-call | tf_op jit(solution)/shard_map/compact/pallas_call | solution.py:378
  49.9 0.1 collective-permute-start.1
  50.0 1.1 %score_own.3.part_ref = f32[768,128]{1,0:T(8,128)S(1)} custom-call(bf16[784,768]{1,0:T(8,128)(2,1)S(1)} %get-tuple-element.90.own_ref, bf16[768,128]{1,0:T(8,128)(2,1)S(1)} %get-tuple-element.91.tags_ref), custom_call_target="tpu_custom_call" | custom-call | flops 905969664 | bytes 1179648 | tf_op jit(solution)/shard_map/score_own/pallas_call | solution.py:395
  51.1 1.7 %collective-permute-done.1.other_ref = bf16[784,768]{1,0:T(8,128)(2,1)S(1)} collective-permute-done((bf16[784,768]{1,0:T(8,128)(2,1)S(1)}, bf16[784,768]{1,0:T(8,128)(2,1)S(1)}, u32[]{:S(2)}, u32[]{:S(2)}) %collective-permute-start.1) | collective-permute-done | bytes 1204256 | tf_op jit(solution)/shard_map/ppermute | solution.py:394
  52.9 1.5 %score_other.3 = f32[64,128]{1,0:T(8,128)S(1)} custom-call(s32[8,1536]{1,0:T(8,128)S(1)} %get-tuple-element.89.pos_ref, bf16[784,768]{1,0:T(8,128)(2,1)S(1)} %get-tuple-element.90.own_ref, bf16[768,128]{1,0:T(8,128)(2,1)S(1)} %get-tuple-element.91.tags_ref, bf16[784,768]{1,0:T(8,128)(2,1)S(1)} %collective-permute-done.1.other_ref, ...), custom_call_target="tpu_custom_call" | custom-call | tf_op jit(solution)/shard_map/score_other/pallas_call | solution.py:408
  54.4 14.4 %all_to_all.70 = f32[64,1,128]{2,1,0:T(1,128)S(1)} all-to-all(f32[64,1,128]{2,1,0:T(1,128)S(1)} %bitcast.70), channel_id=1, replica_groups=mesh['yx'=16,'core'=2,'z'=4] {'yx','z'}, dimensions={0} | all-to-all | bytes 65536 | tf_op jit(solution)/shard_map/all_to_all | solution.py:360
  68.8 1.0 %answer.3 = (f32[1,512]{1,0:T(1,128)}, s32[1]{0:T(128)}) custom-call(s32[8,512]{1,0:T(8,128)S(1)} %get-tuple-element.87.where_ref, f32[64,128]{1,0:T(8,128)S(1)} %bitcast.73), custom_call_target="tpu_custom_call" | custom-call | tf_op jit(solution)/shard_map/answer/pallas_call | solution.py:417
  69.8 0.0 copy-done
  69.8 0.0 copy-done.1
  70.5 0.2 conditional.2
Async XLA Ops:
  47.6 22.2 %copy-start = (bf16[512,768]{1,0:T(8,128)(2,1)S(1)}, bf16[512,768]{1,0:T(8,128)(2,1)}, u32[]{:S(2)}) copy-start(bf16[512,768]{1,0:T(8,128)(2,1)} %rows_ref.1) | copy-start | bytes 2359300
  47.6 22.2 %copy-start.1 = (s32[512]{0:T(512)S(1)}, s32[512]{0:T(512)}, u32[]{:S(2)}) copy-start(s32[512]{0:T(512)} %param.9) | copy-start | bytes 6148
  49.9 3.0 %collective-permute-start.1 = (bf16[784,768]{1,0:T(8,128)(2,1)S(1)}, bf16[784,768]{1,0:T(8,128)(2,1)S(1)}, u32[]{:S(2)}, u32[]{:S(2)}) collective-permute-start(bf16[784,768]{1,0:T(8,128)(2,1)S(1)} %get-tuple-element.90.own_ref), channel_id=1, source_target_pairs={{0,4},{4,0},{1,5},{5,1},{2,6},{6,2},{3,7},{7,3},{8,12},{12,8},{9,1... | collective-permute-start | bytes 3612680 | tf_op jit(solution)/shard_map/ppermute | solution.py:394

commit v3 on v2

--- a/solution.py
+++ b/solution.py
@@ -22,6 +22,7 @@
 ALIGN = 16
 COLS = 256
 HEAVY_LOAD = 72
+SEND_PARTS = 4
 
 F32 = jnp.float32
 BF16 = jnp.bfloat16
@@ -32,6 +33,7 @@
     slots: int
     shift: tuple
     chunk: int
+    window: int
     capacity: int
     step: int
     sized: bool
@@ -57,8 +59,8 @@
         return self.slots * (lax.axis_index("yx") * 4 + lax.axis_index("z"))
 
 
-TIGHT = Plan(24, (2731, 16), 384, 768, 384, True)
-ROOMY = Plan(32, (1, 5), 256, 1280, 320, False)
+TIGHT = Plan(24, (2731, 16), 384, 256, 768, 384, True)
+ROOMY = Plan(32, (1, 5), 256, 272, 1280, 320, False)
 
 
 def iota(shape, dim):
@@ -95,7 +97,9 @@
     theirs = size_class(count_row, index_row)
     ahead = (theirs > mine) | ((theirs == mine) & (index_row < index))
     order = jnp.sum(ahead.astype(F32), axis=1, keepdims=True).astype(I32)
-    ends = [jnp.sum((mine >= least).astype(F32)).astype(I32) for least in (3, 2, 1)]
+    coded = jnp.where(mine >= 3, 1.0, 0.0) + jnp.where(mine >= 2, 64.0, 0.0)
+    coded = jnp.sum(coded + jnp.where(mine >= 1, 4096.0, 0.0)).astype(I32)
+    ends = [coded & 63, (coded >> 6) & 63, coded >> 12]
     loads = [jnp.int32(0), jnp.int32(0), jnp.int32(0), jnp.int32(HEAVY_LOAD)]
     taken = [jnp.int32(0), jnp.int32(0), jnp.int32(0), jnp.int32(1)]
     code = jnp.full((GROUPS, 1), 3 * 32, I32)
@@ -106,13 +110,14 @@
             )
         else:
             weight = jnp.int32(14)
-        least, kind = loads[0], jnp.int32(0)
+        first = loads[1] < loads[0]
+        last = loads[3] < loads[2]
+        low = jnp.where(first, loads[1], loads[0])
+        high = jnp.where(last, loads[3], loads[2])
+        kind = jnp.where(high < low, jnp.where(last, 3, 2), jnp.where(first, 1, 0))
         place = taken[0]
         for other in range(1, KINDS):
-            better = loads[other] < least
-            least = jnp.where(better, loads[other], least)
-            kind = jnp.where(better, other, kind)
-            place = jnp.where(better, taken[other], place)
+            place = jnp.where(kind == other, taken[other], place)
         for other in range(KINDS):
             chosen = kind == other
             loads[other] = loads[other] + jnp.where(chosen, weight, 0)
@@ -164,9 +169,10 @@
     note = jnp.sum(jnp.where(shown, code_of_group, 0.0), axis=0, keepdims=True)
     note = jnp.where(iota((1, 128), 1) == 0, flag, note)
     meta = jnp.concatenate([tags, jnp.broadcast_to(note, (CHIPS, LANES))], axis=1)
-    blocks = plan.chunk // plan.slots
-    for first in range(0, plan.held, plan.chunk):
-        row = iota((plan.chunk, ROWS), 0) + first
+    part = plan.held // SEND_PARTS
+    blocks = part // plan.slots
+    for first in range(0, plan.held, part):
+        row = iota((part, ROWS), 0) + first
         out = jnp.dot((row == flat).astype(BF16), normed, preferred_element_type=F32)
         noted = []
         for block in range(blocks):
@@ -177,7 +183,7 @@
             noted.append(out[end - 8 : end, : 2 * LANES] + last)
         noted = jnp.concatenate(noted, axis=0)
         out = jnp.concatenate([noted, out[:, 2 * LANES :]], axis=1)
-        out_ref[pl.ds(first, plan.chunk), :] = out.astype(BF16)
+        out_ref[pl.ds(first, part), :] = out.astype(BF16)
 
 
 def compact_kernel(plan, held_ref, out_ref, tags_ref, pos_ref, total_ref, tag_ref):
@@ -192,9 +198,9 @@
     note_top = jnp.max(meta[:, LANES:], axis=0, keepdims=True)
     note_low = jnp.min(meta[:, LANES:], axis=0, keepdims=True)
     note_lane = iota((1, 128), 1)
-    flag = jnp.max(
-        jnp.where(note_lane == 0, note_top, jnp.where(note_lane >= 32, note_top - note_low, 0.0))
-    )
+    flag = jnp.where(note_lane == 0, note_top, 0.0)
+    flag = jnp.where(note_lane >= 32, note_top - note_low, flag)
+    flag = jnp.max(flag, axis=1, keepdims=True)
     count = jnp.sum((tags > 0).astype(F32), axis=1, keepdims=True)
     before = (iota((CHIPS, CHIPS), 1) < iota((CHIPS, CHIPS), 0)).astype(BF16)
     offset = jnp.dot(
@@ -209,7 +215,13 @@
     offset_row = jnp.sum(jnp.where(own_block, offset, 0.0), axis=0, keepdims=True).astype(I32)
     pos = jnp.where(tag_row > 0, offset_row + plan.slot_of(iota((1, held), 1)), -1)
     pos_ref[...] = jnp.broadcast_to(pos, (8, held))
-    total = jnp.sum(count).astype(I32)
+    per_chunk = plan.chunk // plan.slots
+    ahead = iota((CHIPS, LANES), 0) - iota((CHIPS, LANES), 1) * per_chunk
+    filled = jnp.where((ahead >= 0) & (ahead < per_chunk), count, 0.0)
+    filled = jnp.sum(filled, axis=0, keepdims=True)
+    total = jnp.sum(filled, axis=1, keepdims=True)
+    over = jnp.max(filled, axis=1, keepdims=True) > plan.window - ALIGN
+    over = over | (total > plan.capacity)
     source = iota((CHIPS, 1), 0)
     total_ref[pl.ds(0, ALIGN), :] = jnp.zeros((ALIGN, WIDTH), BF16)
     tag_ref[pl.ds(0, ALIGN), :] = jnp.zeros((ALIGN, LANES), BF16)
@@ -220,12 +232,12 @@
             low = jnp.sum(jnp.where(source == first // plan.slots, offset, 0.0)).astype(I32)
             base = pl.multiple_of((low >> 4) << 4, ALIGN)
         lanes = slice(first, first + chunk)
-        take = (iota((chunk + ALIGN, chunk), 0) + base) == pos[:, lanes]
+        take = (iota((plan.window, chunk), 0) + base) == pos[:, lanes]
         part = jnp.dot(take.astype(BF16), held_ref[lanes, :], preferred_element_type=F32)
         tag = jnp.sum(jnp.where(take, tag_row[:, lanes], 0.0), axis=1, keepdims=True)
-        tag = jnp.broadcast_to(tag, (chunk + ALIGN, LANES)).astype(BF16)
+        tag = jnp.broadcast_to(tag, (plan.window, LANES)).astype(BF16)
         part = part.astype(BF16)
-        head, rest = pl.ds(base, ALIGN), pl.ds(base + ALIGN, chunk)
+        head, rest = pl.ds(base, ALIGN), pl.ds(base + ALIGN, plan.window - ALIGN)
         total_ref[head, :] += part[:ALIGN]
         total_ref[rest, :] = part[ALIGN:]
         tag_ref[head, :] += tag[:ALIGN]
@@ -237,7 +249,7 @@
         tag_ref[rows, :] = jnp.zeros((ALIGN, LANES), BF16)
         return carry
 
-    lax.fori_loop((base + chunk + ALIGN) >> 4, plan.capacity // ALIGN, clear, 0)
+    lax.fori_loop((base + plan.window) >> 4, plan.capacity // ALIGN, clear, 0)
     out_ref[pl.ds(0, plan.capacity), :] = total_ref[pl.ds(0, plan.capacity), :]
     tags = tag_ref[pl.ds(0, plan.capacity), :]
     tags_ref[...] = tags
@@ -245,7 +257,7 @@
     tag_lanes = lax.dot_general(
         one_lane, tags, (((1,), (1,)), ((), ())), preferred_element_type=F32
     )
-    flag = jnp.maximum(flag, (total > plan.capacity).astype(F32))
+    flag = jnp.maximum(flag, over.astype(F32))
     note = jnp.where(note_lane == 0, flag, jnp.where(note_lane >= 32, note_top, 0.0))
     note = jnp.concatenate([note, jnp.zeros((1, plan.capacity - LANES), F32)], axis=1)
     tail = jnp.where(iota((TAIL, plan.capacity), 0) < TAIL // 2, note, tag_lanes)
@@ -324,14 +336,16 @@
     chip = where_ref[0:1, :]
     lane = where_ref[1:2, :]
     back = back_ref[...]
-    to_chip = (iota((CHIPS, ROWS), 0) == chip).astype(F32)
+    to_chip = (iota((CHIPS, ROWS), 0) == chip).astype(BF16)
+    high = back.astype(BF16)
+    rest = back - high.astype(F32)
+    middle = rest.astype(BF16)
+    low = (rest - middle.astype(F32)).astype(BF16)
+    parts = jnp.concatenate([high, middle, low], axis=1)
     by_row = lax.dot_general(
-        back,
-        to_chip,
-        (((0,), (0,)), ((), ())),
-        preferred_element_type=F32,
-        precision=lax.Precision.HIGHEST,
-    )
+        parts, to_chip, (((0,), (0,)), ((), ())), preferred_element_type=F32
+    )
+    by_row = (by_row[:LANES] + by_row[LANES : 2 * LANES]) + by_row[2 * LANES :]
     at_lane = iota((LANES, ROWS), 0) == lane
     out_ref[...] = jnp.sum(jnp.where(at_lane, by_row, 0.0), axis=0, keepdims=True)
     last = iota((CHIPS, LANES), 1) == ((plan.first_lane() + plan.slots - 1) & (LANES - 1))
@@ -387,8 +401,8 @@
         in_specs=[VMEM],
         out_specs=(VMEM, VMEM, VMEM),
         scratch_shapes=[
-            pltpu.VMEM((plan.held + plan.chunk + ALIGN, WIDTH), BF16),
-            pltpu.VMEM((plan.held + plan.chunk + ALIGN, LANES), BF16),
+            pltpu.VMEM((plan.held + plan.window, WIDTH), BF16),
+            pltpu.VMEM((plan.held + plan.window, LANES), BF16),
         ],
     )(held)
     other = lax.ppermute(packed, "core", [(0, 1), (1, 0)])

time: 71.1 us -> 70.5 us (level)
  no operation moved by 1% of the time
where the time goes in v3:
time: 70.5 us; the launch traced here: 70.3 us
  blocking collectives  58.7 us (83%)
  Pallas kernels  8.51 us (12%)
  waiting for transfers between devices  1.74 us (2%)
  between operations  1 us (1%)
    all_to_all x2, blocking collectives, swap(): lax.all_to_all(message, ('yx', 'z'), split_axis=0, concat_axis=0, tiled=T...  58.7 us
    pallas_call x1, Pallas kernels, owner_path(): call(send_kernel, plan, 'send', out_shape=(shape((plan.held, WIDTH), BF16...  3.27 us
    ppermute x1, waiting for transfers between devices, owner_path(): other = lax.ppermute(packed, 'core', [(0, 1), (1, 0)])  1.74 us
    pallas_call x1, Pallas kernels, owner_path(): call(compact_kernel, plan, 'compact', out_shape=(shape((plan.capacity + p...  1.73 us
    pallas_call x1, Pallas kernels, owner_path(): call(other_kernel, plan, 'score_other', out_shape=shape((CHIPS, LANES), F...  1.5 us
  transfers between devices with their start and end apart: 1, of which 1 were waited for; matrix products, arithmetic and copies ran while one was open for 0% of the time, Pallas kernels for 2%

profile of v3, /device:TPU:0, one launch (start us, length us, event | category | flops | bytes accessed | tf_op | source)
XLA Modules:
  0.0 70.3 jit_solution(1366168912750294871)
XLA Ops:
  0.0 3.3 %send.3 = (bf16[1536,768]{1,0:T(8,128)(2,1)S(1)}, s32[8,512]{1,0:T(8,128)S(1)}) custom-call(s32[1,512]{1,0:T(1,128)} %bitcast.83, bf16[512,768]{1,0:T(8,128)(2,1)} %rows_ref.1), custom_call_target="tpu_custom_call" | custom-call | tf_op jit(solution)/shard_map/send/pallas_call | solution.py:378
  3.3 44.3 %all_to_all.69 = bf16[64,24,768]{2,1,0:T(8,128)(2,1)S(1)} all-to-all(bf16[64,24,768]{2,1,0:T(8,128)(2,1)S(1)} %bitcast.69), channel_id=1, replica_groups=mesh['yx'=16,'core'=2,'z'=4] {'yx','z'}, dimensions={0} | all-to-all | bytes 4718592 | tf_op jit(solution)/shard_map/all_to_all | solution.py:374
  47.6 0.0 copy-start
  47.6 0.0 copy-start.1
  47.6 1.7 %compact.3 = (bf16[784,768]{1,0:T(8,128)(2,1)S(1)}, bf16[768,128]{1,0:T(8,128)(2,1)S(1)}, s32[8,1536]{1,0:T(8,128)S(1)}) custom-call(bf16[1536,768]{1,0:T(8,128)(2,1)S(1)} %bitcast.67), custom_call_target="tpu_custom_call" | custom-call | tf_op jit(solution)/shard_map/compact/pallas_call | solution.py:392
  49.4 0.1 collective-permute-start.1
  49.5 1.1 %score_own.3.part_ref = f32[768,128]{1,0:T(8,128)S(1)} custom-call(bf16[784,768]{1,0:T(8,128)(2,1)S(1)} %get-tuple-element.90.own_ref, bf16[768,128]{1,0:T(8,128)(2,1)S(1)} %get-tuple-element.91.tags_ref), custom_call_target="tpu_custom_call" | custom-call | flops 905969664 | bytes 1179648 | tf_op jit(solution)/shard_map/score_own/pallas_call | solution.py:409
  50.6 1.7 %collective-permute-done.1.other_ref = bf16[784,768]{1,0:T(8,128)(2,1)S(1)} collective-permute-done((bf16[784,768]{1,0:T(8,128)(2,1)S(1)}, bf16[784,768]{1,0:T(8,128)(2,1)S(1)}, u32[]{:S(2)}, u32[]{:S(2)}) %collective-permute-start.1) | collective-permute-done | bytes 1204256 | tf_op jit(solution)/shard_map/ppermute | solution.py:408
  52.4 1.5 %score_other.3 = f32[64,128]{1,0:T(8,128)S(1)} custom-call(s32[8,1536]{1,0:T(8,128)S(1)} %get-tuple-element.89.pos_ref, bf16[784,768]{1,0:T(8,128)(2,1)S(1)} %get-tuple-element.90.own_ref, bf16[768,128]{1,0:T(8,128)(2,1)S(1)} %get-tuple-element.91.tags_ref, bf16[784,768]{1,0:T(8,128)(2,1)S(1)} %collective-permute-done.1.other_ref, ...), custom_call_target="tpu_custom_call" | custom-call | tf_op jit(solution)/shard_map/score_other/pallas_call | solution.py:422
  53.9 14.4 %all_to_all.70 = f32[64,1,128]{2,1,0:T(1,128)S(1)} all-to-all(f32[64,1,128]{2,1,0:T(1,128)S(1)} %bitcast.70), channel_id=1, replica_groups=mesh['yx'=16,'core'=2,'z'=4] {'yx','z'}, dimensions={0} | all-to-all | bytes 65536 | tf_op jit(solution)/shard_map/all_to_all | solution.py:374
  68.3 0.9 %answer.3 = (f32[1,512]{1,0:T(1,128)}, s32[1]{0:T(128)}) custom-call(s32[8,512]{1,0:T(8,128)S(1)} %get-tuple-element.87.where_ref, f32[64,128]{1,0:T(8,128)S(1)} %bitcast.73), custom_call_target="tpu_custom_call" | custom-call | tf_op jit(solution)/shard_map/answer/pallas_call | solution.py:431
  69.1 0.0 copy-done
  69.2 0.0 copy-done.1
  69.9 0.2 conditional.2
Async XLA Ops:
  47.6 21.6 %copy-start = (bf16[512,768]{1,0:T(8,128)(2,1)S(1)}, bf16[512,768]{1,0:T(8,128)(2,1)}, u32[]{:S(2)}) copy-start(bf16[512,768]{1,0:T(8,128)(2,1)} %rows_ref.1) | copy-start | bytes 2359300
  47.6 21.6 %copy-start.1 = (s32[512]{0:T(512)S(1)}, s32[512]{0:T(512)}, u32[]{:S(2)}) copy-start(s32[512]{0:T(512)} %param.9) | copy-start | bytes 6148
  49.4 3.0 %collective-permute-start.1 = (bf16[784,768]{1,0:T(8,128)(2,1)S(1)}, bf16[784,768]{1,0:T(8,128)(2,1)S(1)}, u32[]{:S(2)}, u32[]{:S(2)}) collective-permute-start(bf16[784,768]{1,0:T(8,128)(2,1)S(1)} %get-tuple-element.90.own_ref), channel_id=1, source_target_pairs={{0,4},{4,0},{1,5},{5,1},{2,6},{6,2},{3,7},{7,3},{8,12},{12,8},{9,1... | collective-permute-start | bytes 3612680 | tf_op jit(solution)/shard_map/ppermute | solution.py:408

commit v4 on v3

--- a/solution.py
+++ b/solution.py
@@ -67,7 +67,7 @@
     return lax.broadcasted_iota(I32, shape, dim)
 
 
-def deal(plan, group_hit):
+def deal(plan, group_hit, meanwhile):
     count = jnp.sum(group_hit, axis=1, keepdims=True)
     count_row = lax.dot_general(
         jnp.ones((8, ROWS), BF16),
@@ -100,6 +100,7 @@
     coded = jnp.where(mine >= 3, 1.0, 0.0) + jnp.where(mine >= 2, 64.0, 0.0)
     coded = jnp.sum(coded + jnp.where(mine >= 1, 4096.0, 0.0)).astype(I32)
     ends = [coded & 63, (coded >> 6) & 63, coded >> 12]
+    other_work = meanwhile()
     loads = [jnp.int32(0), jnp.int32(0), jnp.int32(0), jnp.int32(HEAVY_LOAD)]
     taken = [jnp.int32(0), jnp.int32(0), jnp.int32(0), jnp.int32(1)]
     code = jnp.full((GROUPS, 1), 3 * 32, I32)
@@ -123,7 +124,7 @@
             loads[other] = loads[other] + jnp.where(chosen, weight, 0)
             taken[other] = taken[other] + jnp.where(chosen, 1, 0)
         code = jnp.where(order == turn, kind * 32 + place, code)
-    return code, unsure
+    return code, unsure, other_work
 
 
 def send_kernel(plan, ids_ref, rows_ref, out_ref, where_ref, my_ids, my_rows, arrived):
@@ -135,7 +136,14 @@
     ids = my_ids[...]
     inner = ids & 15
     hit = iota((GROUPS, ROWS), 0) == (ids >> 4)
-    code_of_group, unsure = deal(plan, hit.astype(F32))
+
+    def normalise():
+        fetch_rows.wait()
+        wide = my_rows[...].astype(F32)
+        scale = lax.rsqrt(jnp.sum(wide * wide, axis=1, keepdims=True) + 1e-6)
+        return (wide * scale).astype(BF16)
+
+    code_of_group, unsure, normed = deal(plan, hit.astype(F32), normalise)
     code_of_group = code_of_group.astype(F32)
     code = jnp.sum(jnp.where(hit, code_of_group, 0.0), axis=0, keepdims=True).astype(I32)
     kind, place = code >> 5, code & 31
@@ -157,17 +165,15 @@
     lost = jnp.max(over.astype(F32), axis=1, keepdims=True)
     flag = jnp.maximum(lost, unsure.astype(F32))
 
-    fetch_rows.wait()
-    wide = my_rows[...].astype(F32)
-    scale = lax.rsqrt(jnp.sum(wide * wide, axis=1, keepdims=True) + 1e-6)
-    normed = (wide * scale).astype(BF16)
-
     at_lane = (iota((LANES, ROWS), 0) == lane).astype(BF16)
     tagged = (to_chip * (place + 1).astype(F32)).astype(BF16)
     tags = lax.dot_general(tagged, at_lane, (((1,), (1,)), ((), ())), preferred_element_type=F32)
     shown = iota((GROUPS, 128), 1) == iota((GROUPS, 128), 0) + 32
     note = jnp.sum(jnp.where(shown, code_of_group, 0.0), axis=0, keepdims=True)
-    note = jnp.where(iota((1, 128), 1) == 0, flag, note)
+    sent = jnp.sum(to_chip, axis=1, keepdims=True)
+    shown = iota((CHIPS, LANES), 1) == iota((CHIPS, LANES), 0) + 64
+    note += jnp.sum(jnp.where(shown, sent, 0.0), axis=0, keepdims=True)
+    note = jnp.where(iota((1, LANES), 1) == 0, flag, note)
     meta = jnp.concatenate([tags, jnp.broadcast_to(note, (CHIPS, LANES))], axis=1)
     part = plan.held // SEND_PARTS
     blocks = part // plan.slots
@@ -186,7 +192,7 @@
         out_ref[pl.ds(first, part), :] = out.astype(BF16)
 
 
-def compact_kernel(plan, held_ref, out_ref, tags_ref, pos_ref, total_ref, tag_ref):
+def compact_kernel(plan, held_ref, out_ref, tags_ref, pos_ref, note_ref, total_ref, tag_ref):
     held = plan.held
     rows = []
     for source in range(CHIPS):
@@ -197,10 +203,18 @@
     tags = meta[:, :LANES]
     note_top = jnp.max(meta[:, LANES:], axis=0, keepdims=True)
     note_low = jnp.min(meta[:, LANES:], axis=0, keepdims=True)
-    note_lane = iota((1, 128), 1)
+    note_lane = iota((1, LANES), 1)
+    per_chunk = plan.chunk // plan.slots
+    filled = jnp.sum(meta[:, LANES:].reshape(CHIPS // per_chunk, per_chunk, LANES), axis=1)
+    total = jnp.sum(filled, axis=0, keepdims=True)
+    filled = jnp.max(filled, axis=0, keepdims=True)
+    over = (filled > plan.window - ALIGN) | (total > plan.capacity)
     flag = jnp.where(note_lane == 0, note_top, 0.0)
-    flag = jnp.where(note_lane >= 32, note_top - note_low, flag)
+    flag = jnp.where((note_lane >= 32) & (note_lane < 64), note_top - note_low, flag)
+    flag = jnp.where(note_lane >= 64, over.astype(F32), flag)
     flag = jnp.max(flag, axis=1, keepdims=True)
+    note = jnp.where(note_lane == 0, flag, jnp.where(note_lane < 64, note_top, 0.0))
+    note_ref[...] = jnp.broadcast_to(note, (8, LANES))
     count = jnp.sum((tags > 0).astype(F32), axis=1, keepdims=True)
     before = (iota((CHIPS, CHIPS), 1) < iota((CHIPS, CHIPS), 0)).astype(BF16)
     offset = jnp.dot(
@@ -215,13 +229,6 @@
     offset_row = jnp.sum(jnp.where(own_block, offset, 0.0), axis=0, keepdims=True).astype(I32)
     pos = jnp.where(tag_row > 0, offset_row + plan.slot_of(iota((1, held), 1)), -1)
     pos_ref[...] = jnp.broadcast_to(pos, (8, held))
-    per_chunk = plan.chunk // plan.slots
-    ahead = iota((CHIPS, LANES), 0) - iota((CHIPS, LANES), 1) * per_chunk
-    filled = jnp.where((ahead >= 0) & (ahead < per_chunk), count, 0.0)
-    filled = jnp.sum(filled, axis=0, keepdims=True)
-    total = jnp.sum(filled, axis=1, keepdims=True)
-    over = jnp.max(filled, axis=1, keepdims=True) > plan.window - ALIGN
-    over = over | (total > plan.capacity)
     source = iota((CHIPS, 1), 0)
     total_ref[pl.ds(0, ALIGN), :] = jnp.zeros((ALIGN, WIDTH), BF16)
     tag_ref[pl.ds(0, ALIGN), :] = jnp.zeros((ALIGN, LANES), BF16)
@@ -257,25 +264,28 @@
     tag_lanes = lax.dot_general(
         one_lane, tags, (((1,), (1,)), ((), ())), preferred_element_type=F32
     )
-    flag = jnp.maximum(flag, over.astype(F32))
-    note = jnp.where(note_lane == 0, flag, jnp.where(note_lane >= 32, note_top, 0.0))
-    note = jnp.concatenate([note, jnp.zeros((1, plan.capacity - LANES), F32)], axis=1)
-    tail = jnp.where(iota((TAIL, plan.capacity), 0) < TAIL // 2, note, tag_lanes)
     for first in range(0, plan.capacity, WIDTH):
-        piece = tail[:, first : first + WIDTH].astype(BF16)
+        piece = tag_lanes[:, first : first + WIDTH].astype(BF16)
         out_ref[pl.ds(plan.capacity + first // WIDTH * TAIL, TAIL), : piece.shape[1]] = piece
 
 
-def tail_of(plan, ref):
+def row_tags(plan, ref):
     pieces = []
     for first in range(0, plan.capacity, WIDTH):
         rows = pl.ds(plan.capacity + first // WIDTH * TAIL, TAIL)
         pieces.append(ref[rows, : min(WIDTH, plan.capacity - first)].astype(F32))
-    tail = jnp.concatenate(pieces, axis=1)
-    return tail[:1, :LANES], tail[TAIL // 2 : TAIL // 2 + 1, :]
-
-
-def score_block(plan, own_ref, tags_ref, rows_ref, row_tags, start, best, same):
+    return jnp.concatenate(pieces, axis=1)[:1]
+
+
+def flag_kernel(plan, own_ref, other_ref, flag_ref):
+    own, other = own_ref[...], other_ref[...]
+    lane = iota((8, LANES), 1)
+    raised = jnp.where(lane == 0, jnp.maximum(own, other), 0.0)
+    raised = jnp.where((lane >= 32) & (own != other), 1.0, raised)
+    flag_ref[0] = (jnp.max(raised) > 0.0).astype(I32)
+
+
+def score_block(plan, own_ref, tags_ref, rows_ref, their_tags, start, best, same):
     own = own_ref[pl.ds(start, plan.step), :]
     own_tag = tags_ref[pl.ds(start, plan.step), :1].astype(F32)
     for first in range(0, plan.capacity, COLS):
@@ -283,7 +293,7 @@
         scores = lax.dot_general(
             own, rows, (((1,), (1,)), ((), ())), preferred_element_type=F32
         )
-        match = own_tag == row_tags[:, first : first + COLS]
+        match = own_tag == their_tags[:, first : first + COLS]
         if same:
             index = iota((plan.step, COLS), 0) + (start - first)
             match = match & (index != iota((plan.step, COLS), 1))
@@ -294,20 +304,15 @@
 
 
 def own_kernel(plan, own_ref, tags_ref, out_ref):
-    _, own_tags = tail_of(plan, own_ref)
+    own_tags = row_tags(plan, own_ref)
     for start in range(0, plan.capacity, plan.step):
         best = jnp.full((plan.step, LANES), -1.0, F32)
         best = score_block(plan, own_ref, tags_ref, own_ref, own_tags, start, best, True)
         out_ref[pl.ds(start, plan.step), :] = best
 
 
-def other_kernel(plan, pos_ref, own_ref, tags_ref, other_ref, part_ref, out_ref):
-    own_note, _ = tail_of(plan, own_ref)
-    other_note, other_tags = tail_of(plan, other_ref)
-    note_lane = iota((1, LANES), 1)
-    differs = (note_lane >= 32) & (own_note != other_note)
-    raised = jnp.where(note_lane == 0, jnp.maximum(own_note, other_note), 0.0)
-    flag = jnp.max(jnp.where(differs, 1.0, raised), axis=1, keepdims=True)
+def other_kernel(plan, pos_ref, own_ref, tags_ref, other_ref, part_ref, _, out_ref):
+    other_tags = row_tags(plan, other_ref)
     found = [jnp.zeros((8, plan.chunk), F32)] * (plan.held // plan.chunk)
     for start in range(0, plan.capacity, plan.step):
         best = part_ref[pl.ds(start, plan.step), :]
@@ -323,7 +328,6 @@
     for index, values in enumerate(found):
         lane = iota((1, plan.chunk), 1)
         values = jnp.sum(values, axis=0, keepdims=True)
-        values = jnp.where(plan.slot_of(lane) == plan.slots - 1, flag, values)
         in_block = plan.block_of(lane) == iota((blocks, plan.chunk), 0)
         mine = jnp.where(in_block, values, 0.0)
         folded = mine[:, :LANES]
@@ -332,7 +336,7 @@
         out_ref[index * blocks : (index + 1) * blocks, :] = folded
 
 
-def answer_kernel(plan, where_ref, back_ref, out_ref, flag_ref):
+def answer_kernel(plan, where_ref, back_ref, out_ref):
     chip = where_ref[0:1, :]
     lane = where_ref[1:2, :]
     back = back_ref[...]
@@ -348,8 +352,6 @@
     by_row = (by_row[:LANES] + by_row[LANES : 2 * LANES]) + by_row[2 * LANES :]
     at_lane = iota((LANES, ROWS), 0) == lane
     out_ref[...] = jnp.sum(jnp.where(at_lane, by_row, 0.0), axis=0, keepdims=True)
-    last = iota((CHIPS, LANES), 1) == ((plan.first_lane() + plan.slots - 1) & (LANES - 1))
-    flag_ref[0] = (jnp.max(jnp.where(last, back, 0.0)) > 0.0).astype(I32)
 
 
 VMEM = pl.BlockSpec(memory_space=pltpu.VMEM)
@@ -389,7 +391,7 @@
         ],
     )(cluster_ids.reshape(1, ROWS), embeddings)
     held = swap(plan, message)
-    packed, tags, pos = call(
+    packed, tags, pos, note = call(
         compact_kernel,
         plan,
         "compact",
@@ -397,15 +399,18 @@
             shape((plan.capacity + plan.tail, WIDTH), BF16),
             shape((plan.capacity, LANES), BF16),
             shape((8, plan.held), I32),
+            shape((8, LANES), F32),
         ),
         in_specs=[VMEM],
-        out_specs=(VMEM, VMEM, VMEM),
+        out_specs=(VMEM,) * 4,
         scratch_shapes=[
             pltpu.VMEM((plan.held + plan.window, WIDTH), BF16),
             pltpu.VMEM((plan.held + plan.window, LANES), BF16),
         ],
     )(held)
-    other = lax.ppermute(packed, "core", [(0, 1), (1, 0)])
+    pairs = [(0, 1), (1, 0)]
+    other_note = lax.ppermute(note, "core", pairs)
+    other = lax.ppermute(packed, "core", pairs)
     part = call(
         own_kernel,
         plan,
@@ -419,24 +424,33 @@
             transcendentals=0,
         ),
     )(packed, tags)
+    flag = call(
+        flag_kernel,
+        plan,
+        "flag",
+        out_shape=shape((1,), I32),
+        in_specs=[VMEM, VMEM],
+        out_specs=SMEM,
+    )(note, other_note)
+    flag = lax.clamp(0, flag[0], 1)
     best = call(
         other_kernel,
         plan,
         "score_other",
         out_shape=shape((CHIPS, LANES), F32),
-        in_specs=[VMEM] * 5,
+        in_specs=[VMEM] * 5 + [pl.BlockSpec(memory_space=pl.ANY)],
         out_specs=VMEM,
-    )(pos, packed, tags, other, part)
+    )(pos, packed, tags, other, part, flag.reshape(1))
     back = swap(plan, best)
-    answer, flag = call(
+    answer = call(
         answer_kernel,
         plan,
         "answer",
-        out_shape=(shape((1, ROWS), F32), shape((1,), I32)),
-        in_specs=[VMEM, VMEM],
-        out_specs=(VMEM, SMEM),
+        out_shape=shape((1, ROWS), F32),
+        in_specs=[VMEM] * 2,
+        out_specs=VMEM,
     )(where, back)
-    return answer.reshape(ROWS), flag[0]
+    return answer.reshape(ROWS), flag
 
 
 def pair_max(left_rows, left_ids, left_pos, right_rows, right_ids, right_pos):
@@ -514,8 +528,8 @@
         return lax.switch(flag, [keep, last_resort], rows, ids, answer)
 
     answer, flag = owner_path(TIGHT, embeddings, cluster_ids)
-    embeddings, cluster_ids, answer, flag = lax.optimization_barrier(
-        (embeddings, cluster_ids, answer, flag)
+    embeddings, cluster_ids, answer = lax.optimization_barrier(
+        (embeddings, cluster_ids, answer)
     )
     return lax.switch(flag, [keep, roomy], embeddings, cluster_ids, answer)
 

time: 70.5 us -> 70.7 us (level)
  Pallas kernels: 8.51 us -> 9.28 us
    pallas_call x1 -> x2, Pallas kernels: 0.89 us -> 1.51 us  [the longest x1 0.87 us: owner_path(): call(answer_kernel, plan, 'answer', out_shape=shape((1, ROWS), F32), in_s...]
    ppermute x1 -> x2, waiting for transfers between devices: 1.74 us -> 1.26 us  [the longest x1 1.25 us: owner_path(): other_note = lax.ppermute(note, 'core', pairs)]
  transfers between devices with their start and end apart: 1 -> 2, of which waited for: 1 -> 1; matrix products, arithmetic and copies ran while one was open for 0% -> 0% of each run, Pallas kernels for 2% -> 2%
where the time goes in v4:
time: 70.7 us; the launch traced here: 70.5 us
  blocking collectives  58.7 us (83%)
  Pallas kernels  9.28 us (13%)
  waiting for transfers between devices  1.26 us (2%)
    all_to_all x2, blocking collectives, swap(): lax.all_to_all(message, ('yx', 'z'), split_axis=0, concat_axis=0, tiled=T...  58.7 us
    pallas_call x1, Pallas kernels, owner_path(): call(send_kernel, plan, 'send', out_shape=(shape((plan.held, WIDTH), BF16...  3.33 us
    pallas_call x1, Pallas kernels, owner_path(): call(compact_kernel, plan, 'compact', out_shape=(shape((plan.capacity + p...  1.84 us
    pallas_call x1, Pallas kernels, owner_path(): call(other_kernel, plan, 'score_other', out_shape=shape((CHIPS, LANES), F...  1.48 us
  transfers between devices with their start and end apart: 2, of which 1 were waited for; matrix products, arithmetic and copies ran while one was open for 0% of the time, Pallas kernels for 2%

profile of v4, /device:TPU:0, one launch (start us, length us, event | category | flops | bytes accessed | tf_op | source)
XLA Modules:
  0.0 70.5 jit_solution(14360351866545791310)
XLA Ops:
  0.0 3.3 %send.3 = (bf16[1536,768]{1,0:T(8,128)(2,1)S(1)}, s32[8,512]{1,0:T(8,128)S(1)}) custom-call(s32[1,512]{1,0:T(1,128)} %bitcast.83, bf16[512,768]{1,0:T(8,128)(2,1)} %rows_ref.1), custom_call_target="tpu_custom_call" | custom-call | tf_op jit(solution)/shard_map/send/pallas_call | solution.py:380
  3.3 44.3 %all_to_all.69 = bf16[64,24,768]{2,1,0:T(8,128)(2,1)S(1)} all-to-all(bf16[64,24,768]{2,1,0:T(8,128)(2,1)S(1)} %bitcast.69), channel_id=1, replica_groups=mesh['yx'=16,'core'=2,'z'=4] {'yx','z'}, dimensions={0} | all-to-all | bytes 4718592 | tf_op jit(solution)/shard_map/all_to_all | solution.py:376
  47.7 0.0 copy-start
  47.7 0.0 copy-start.1
  47.7 1.8 %compact.3 = (bf16[784,768]{1,0:T(8,128)(2,1)S(1)}, bf16[768,128]{1,0:T(8,128)(2,1)S(1)}, s32[8,1536]{1,0:T(8,128)S(1)}, f32[8,128]{1,0:T(8,128)S(1)}) custom-call(bf16[1536,768]{1,0:T(8,128)(2,1)S(1)} %bitcast.67), custom_call_target="tpu_custom_call" | custom-call | tf_op jit(solution)/shard_map/compact/pallas_call | solution.py:394
  49.5 0.1 collective-permute-start.3
  49.6 0.5 collective-permute-start.2
  50.1 1.1 %score_own.3.part_ref = f32[768,128]{1,0:T(8,128)S(1)} custom-call(bf16[784,768]{1,0:T(8,128)(2,1)S(1)} %get-tuple-element.88.own_ref, bf16[768,128]{1,0:T(8,128)(2,1)S(1)} %get-tuple-element.89.tags_ref), custom_call_target="tpu_custom_call" | custom-call | flops 905969664 | bytes 1179648 | tf_op jit(solution)/shard_map/score_own/pallas_call | solution.py:414
  51.2 1.3 %collective-permute-done.2.other_ref = f32[8,128]{1,0:T(8,128)S(1)} collective-permute-done((f32[8,128]{1,0:T(8,128)S(1)}, f32[8,128]{1,0:T(8,128)S(1)}, u32[]{:S(2)}, u32[]{:S(2)}) %collective-permute-start.2) | collective-permute-done | bytes 4128 | tf_op jit(solution)/shard_map/ppermute | solution.py:412
  52.5 0.6 flag.3
  53.8 0.0 collective-permute-done.3.other_ref
  53.8 1.5 %score_other.3 = f32[64,128]{1,0:T(8,128)S(1)} custom-call(s32[8,1536]{1,0:T(8,128)S(1)} %get-tuple-element.87.pos_ref, bf16[784,768]{1,0:T(8,128)(2,1)S(1)} %get-tuple-element.88.own_ref, bf16[768,128]{1,0:T(8,128)(2,1)S(1)} %get-tuple-element.89.tags_ref, bf16[784,768]{1,0:T(8,128)(2,1)S(1)} %collective-permute-done.3.other_ref, ...), custom_call_target="tpu_custom_call" | custom-call | tf_op jit(solution)/shard_map/score_other/pallas_call | solution.py:436
  55.3 14.4 %all_to_all.70 = f32[64,1,128]{2,1,0:T(1,128)S(1)} all-to-all(f32[64,1,128]{2,1,0:T(1,128)S(1)} %bitcast.70), channel_id=1, replica_groups=mesh['yx'=16,'core'=2,'z'=4] {'yx','z'}, dimensions={0} | all-to-all | bytes 65536 | tf_op jit(solution)/shard_map/all_to_all | solution.py:376
  69.7 0.9 %answer.3 = f32[1,512]{1,0:T(1,128)} custom-call(s32[8,512]{1,0:T(8,128)S(1)} %get-tuple-element.86.where_ref, f32[64,128]{1,0:T(8,128)S(1)} %bitcast.73), custom_call_target="tpu_custom_call" | custom-call | tf_op jit(solution)/shard_map/answer/pallas_call | solution.py:445
  70.5 0.0 copy-done
  70.5 0.0 copy-done.1
  (1 shorter events, 0.0 us)
Async XLA Ops:
  47.7 22.9 %copy-start = (bf16[512,768]{1,0:T(8,128)(2,1)S(1)}, bf16[512,768]{1,0:T(8,128)(2,1)}, u32[]{:S(2)}) copy-start(bf16[512,768]{1,0:T(8,128)(2,1)} %rows_ref.1) | copy-start | bytes 2359300
  47.7 22.9 %copy-start.1 = (s32[512]{0:T(512)S(1)}, s32[512]{0:T(512)}, u32[]{:S(2)}) copy-start(s32[512]{0:T(512)} %param.9) | copy-start | bytes 6148
  49.5 4.3 %collective-permute-start.3 = (bf16[784,768]{1,0:T(8,128)(2,1)S(1)}, bf16[784,768]{1,0:T(8,128)(2,1)S(1)}, u32[]{:S(2)}, u32[]{:S(2)}) collective-permute-start(bf16[784,768]{1,0:T(8,128)(2,1)S(1)} %get-tuple-element.88.own_ref), channel_id=1, source_target_pairs={{0,4},{4,0},{1,5},{5,1},{2,6},{6,2},{3,7},{7,3},{8,12},{12,8},{9,1... | collective-permute-start | bytes 3612680 | tf_op jit(solution)/shard_map/ppermute | solution.py:413
  49.6 2.9 %collective-permute-start.2 = (f32[8,128]{1,0:T(8,128)S(1)}, f32[8,128]{1,0:T(8,128)S(1)}, u32[]{:S(2)}, u32[]{:S(2)}) collective-permute-start(f32[8,128]{1,0:T(8,128)S(1)} %get-tuple-element.85.own_ref), channel_id=1, source_target_pairs={{0,4},{4,0},{1,5},{5,1},{2,6},{6,2},{3,7},{7,3},{8,12},{12,8},{9,1... | collective-permute-start | bytes 12296 | tf_op jit(solution)/shard_map/ppermute | solution.py:412

commit v5 on v3

--- a/solution.py
+++ b/solution.py
@@ -502,22 +502,25 @@
     return jnp.max(jnp.where(placement, returned.reshape(total)[:, None], -2.0), axis=0)
 
 
-def body(embeddings, cluster_ids):
-    def keep(rows, ids, done):
-        return done
-
-    def last_resort(rows, ids, done):
-        return any_path(rows, ids)
-
-    def roomy(rows, ids, done):
-        answer, flag = owner_path(ROOMY, rows, ids)
-        return lax.switch(flag, [keep, last_resort], rows, ids, answer)
-
-    answer, flag = owner_path(TIGHT, embeddings, cluster_ids)
+def unless_done(path, embeddings, cluster_ids, answer, flag):
+    def turn(state):
+        rows, ids, _, _ = state
+        return rows, ids, path(rows, ids), jnp.int32(0)
+
     embeddings, cluster_ids, answer, flag = lax.optimization_barrier(
         (embeddings, cluster_ids, answer, flag)
     )
-    return lax.switch(flag, [keep, roomy], embeddings, cluster_ids, answer)
+    state = (embeddings, cluster_ids, answer, flag)
+    return lax.while_loop(lambda state: state[3] > 0, turn, state)[2]
+
+
+def body(embeddings, cluster_ids):
+    def roomy(rows, ids):
+        return unless_done(any_path, rows, ids, *owner_path(ROOMY, rows, ids))
+
+    return unless_done(
+        roomy, embeddings, cluster_ids, *owner_path(TIGHT, embeddings, cluster_ids)
+    )
 
 
 def solution(mesh):

time: 70.5 us -> 70.4 us (level)
  no operation moved by 1% of the time
where the time goes in v5:
time: 70.4 us; the launch traced here: 70.2 us
  blocking collectives  58.7 us (83%)
  Pallas kernels  8.5 us (12%)
  waiting for transfers between devices  1.73 us (2%)
  loops' own time  0.86 us (1%)
    all_to_all x2, blocking collectives, swap(): lax.all_to_all(message, ('yx', 'z'), split_axis=0, concat_axis=0, tiled=T...  58.7 us
    pallas_call x1, Pallas kernels, owner_path(): call(send_kernel, plan, 'send', out_shape=(shape((plan.held, WIDTH), BF16...  3.27 us
    ppermute x1, waiting for transfers between devices, owner_path(): other = lax.ppermute(packed, 'core', [(0, 1), (1, 0)])  1.73 us
    pallas_call x1, Pallas kernels, owner_path(): call(compact_kernel, plan, 'compact', out_shape=(shape((plan.capacity + p...  1.72 us
    pallas_call x1, Pallas kernels, owner_path(): call(other_kernel, plan, 'score_other', out_shape=shape((CHIPS, LANES), F...  1.49 us
  transfers between devices with their start and end apart: 1, of which 1 were waited for; matrix products, arithmetic and copies ran while one was open for 0% of the time, Pallas kernels for 2%

profile of v5, /device:TPU:0, one launch (start us, length us, event | category | flops | bytes accessed | tf_op | source)
XLA Modules:
  0.0 70.2 jit_solution(8112525956129642019)
XLA Ops:
  0.0 3.3 %send.3 = (bf16[1536,768]{1,0:T(8,128)(2,1)S(1)}, s32[8,512]{1,0:T(8,128)S(1)}) custom-call(s32[1,512]{1,0:T(1,128)} %bitcast.14.ids_ref, bf16[512,768]{1,0:T(8,128)(2,1)} %rows_ref.1), custom_call_target="tpu_custom_call" | custom-call | tf_op jit(solution)/shard_map/send/pallas_call | solution.py:378
  3.3 44.3 %all_to_all.68 = bf16[64,24,768]{2,1,0:T(8,128)(2,1)S(1)} all-to-all(bf16[64,24,768]{2,1,0:T(8,128)(2,1)S(1)} %bitcast.84), channel_id=1, replica_groups=mesh['yx'=16,'core'=2,'z'=4] {'yx','z'}, dimensions={0} | all-to-all | bytes 4718592 | tf_op jit(solution)/shard_map/all_to_all | solution.py:374
  47.6 1.7 %compact.3 = (bf16[784,768]{1,0:T(8,128)(2,1)S(1)}, bf16[768,128]{1,0:T(8,128)(2,1)S(1)}, s32[8,1536]{1,0:T(8,128)S(1)}) custom-call(bf16[1536,768]{1,0:T(8,128)(2,1)S(1)} %bitcast.82), custom_call_target="tpu_custom_call" | custom-call | tf_op jit(solution)/shard_map/compact/pallas_call | solution.py:392
  49.4 0.1 collective-permute-start.1
  49.5 1.1 %score_own.3.part_ref = f32[768,128]{1,0:T(8,128)S(1)} custom-call(bf16[784,768]{1,0:T(8,128)(2,1)S(1)} %get-tuple-element.112.own_ref, bf16[768,128]{1,0:T(8,128)(2,1)S(1)} %get-tuple-element.113.tags_ref), custom_call_target="tpu_custom_call" | custom-call | flops 905969664 | bytes 1179648 | tf_op jit(solution)/shard_map/score_own/pallas_call | solution.py:409
  50.6 1.7 %collective-permute-done.1.other_ref = bf16[784,768]{1,0:T(8,128)(2,1)S(1)} collective-permute-done((bf16[784,768]{1,0:T(8,128)(2,1)S(1)}, bf16[784,768]{1,0:T(8,128)(2,1)S(1)}, u32[]{:S(2)}, u32[]{:S(2)}) %collective-permute-start.1) | collective-permute-done | bytes 1204256 | tf_op jit(solution)/shard_map/ppermute | solution.py:408
  52.4 1.5 %score_other.3 = f32[64,128]{1,0:T(8,128)S(1)} custom-call(s32[8,1536]{1,0:T(8,128)S(1)} %get-tuple-element.111.pos_ref, bf16[784,768]{1,0:T(8,128)(2,1)S(1)} %get-tuple-element.112.own_ref, bf16[768,128]{1,0:T(8,128)(2,1)S(1)} %get-tuple-element.113.tags_ref, bf16[784,768]{1,0:T(8,128)(2,1)S(1)} %collective-permute-done.1.other_ref, ...), custom_call_target="tpu_custom_call" | custom-call | tf_op jit(solution)/shard_map/score_other/pallas_call | solution.py:422
  53.9 14.4 %all_to_all.69 = f32[64,1,128]{2,1,0:T(1,128)S(1)} all-to-all(f32[64,1,128]{2,1,0:T(1,128)S(1)} %bitcast.85), channel_id=1, replica_groups=mesh['yx'=16,'core'=2,'z'=4] {'yx','z'}, dimensions={0} | all-to-all | bytes 65536 | tf_op jit(solution)/shard_map/all_to_all | solution.py:374
  68.2 0.9 %answer.3 = (f32[1,512]{1,0:T(1,128)}, s32[1]{0:T(128)}) custom-call(s32[8,512]{1,0:T(8,128)S(1)} %get-tuple-element.109.where_ref, f32[64,128]{1,0:T(8,128)S(1)} %bitcast.86), custom_call_target="tpu_custom_call" | custom-call | tf_op jit(solution)/shard_map/answer/pallas_call | solution.py:431
  69.1 0.9 %while.27 = (f32[512]{0:T(512)}, s32[]{:T(128)}, s32[512]{0:T(512)}, bf16[512,768]{1,0:T(8,128)(2,1)}) while((f32[512]{0:T(512)}, s32[]{:T(128)}, s32[512]{0:T(512)}, bf16[512,768]{1,0:T(8,128)(2,1)}) %tuple.52), condition=%region_12.13_spmd, body=%region_0.12_spmd | while | flops 10608293888 | bytes 95132888 | solution.py:514
Async XLA Ops:
  49.4 3.0 %collective-permute-start.1 = (bf16[784,768]{1,0:T(8,128)(2,1)S(1)}, bf16[784,768]{1,0:T(8,128)(2,1)S(1)}, u32[]{:S(2)}, u32[]{:S(2)}) collective-permute-start(bf16[784,768]{1,0:T(8,128)(2,1)S(1)} %get-tuple-element.112.own_ref), channel_id=1, source_target_pairs={{0,4},{4,0},{1,5},{5,1},{2,6},{6,2},{3,7},{7,3},{8,12},{12,8},{9,1... | collective-permute-start | bytes 3612680 | tf_op jit(solution)/shard_map/ppermute | solution.py:408

commit v6 on v5

--- a/solution.py
+++ b/solution.py
@@ -35,6 +35,7 @@
     chunk: int
     window: int
     capacity: int
+    front: int
     step: int
     sized: bool
 
@@ -59,8 +60,8 @@
         return self.slots * (lax.axis_index("yx") * 4 + lax.axis_index("z"))
 
 
-TIGHT = Plan(24, (2731, 16), 384, 256, 768, 384, True)
-ROOMY = Plan(32, (1, 5), 256, 272, 1280, 320, False)
+TIGHT = Plan(24, (2731, 16), 384, 256, 768, 512, 256, True)
+ROOMY = Plan(32, (1, 5), 256, 272, 1280, 768, 256, False)
 
 
 def iota(shape, dim):
@@ -186,7 +187,7 @@
         out_ref[pl.ds(first, part), :] = out.astype(BF16)
 
 
-def compact_kernel(plan, held_ref, out_ref, tags_ref, pos_ref, total_ref, tag_ref):
+def compact_kernel(plan, held_ref, out_ref, back_ref, tags_ref, pos_ref, total_ref, tag_ref):
     held = plan.held
     rows = []
     for source in range(CHIPS):
@@ -250,7 +251,8 @@
         return carry
 
     lax.fori_loop((base + plan.window) >> 4, plan.capacity // ALIGN, clear, 0)
-    out_ref[pl.ds(0, plan.capacity), :] = total_ref[pl.ds(0, plan.capacity), :]
+    out_ref[pl.ds(0, plan.front), :] = total_ref[pl.ds(0, plan.front), :]
+    back_ref[...] = total_ref[pl.ds(plan.front, plan.capacity - plan.front), :]
     tags = tag_ref[pl.ds(0, plan.capacity), :]
     tags_ref[...] = tags
     one_lane = (iota((TAIL, LANES), 1) == 0).astype(BF16)
@@ -263,29 +265,31 @@
     tail = jnp.where(iota((TAIL, plan.capacity), 0) < TAIL // 2, note, tag_lanes)
     for first in range(0, plan.capacity, WIDTH):
         piece = tail[:, first : first + WIDTH].astype(BF16)
-        out_ref[pl.ds(plan.capacity + first // WIDTH * TAIL, TAIL), : piece.shape[1]] = piece
+        out_ref[pl.ds(plan.front + first // WIDTH * TAIL, TAIL), : piece.shape[1]] = piece
 
 
 def tail_of(plan, ref):
     pieces = []
     for first in range(0, plan.capacity, WIDTH):
-        rows = pl.ds(plan.capacity + first // WIDTH * TAIL, TAIL)
+        rows = pl.ds(plan.front + first // WIDTH * TAIL, TAIL)
         pieces.append(ref[rows, : min(WIDTH, plan.capacity - first)].astype(F32))
     tail = jnp.concatenate(pieces, axis=1)
     return tail[:1, :LANES], tail[TAIL // 2 : TAIL // 2 + 1, :]
 
 
-def score_block(plan, own_ref, tags_ref, rows_ref, row_tags, start, best, same):
-    own = own_ref[pl.ds(start, plan.step), :]
+def score_block(plan, own_refs, tags_ref, rows_ref, count, offset, row_tags, start, best, same):
+    inside = start - plan.front
+    own_ref, at = (own_refs[0], start) if inside < 0 else (own_refs[1], inside)
+    own = own_ref[pl.ds(at, plan.step), :]
     own_tag = tags_ref[pl.ds(start, plan.step), :1].astype(F32)
-    for first in range(0, plan.capacity, COLS):
+    for first in range(0, count, COLS):
         rows = rows_ref[pl.ds(first, COLS), :]
         scores = lax.dot_general(
             own, rows, (((1,), (1,)), ((), ())), preferred_element_type=F32
         )
-        match = own_tag == row_tags[:, first : first + COLS]
+        match = own_tag == row_tags[:, offset + first : offset + first + COLS]
         if same:
-            index = iota((plan.step, COLS), 0) + (start - first)
+            index = iota((plan.step, COLS), 0) + (start - offset - first)
             match = match & (index != iota((plan.step, COLS), 1))
         scores = jnp.where(match, scores, -1.0)
         for lane in range(0, COLS, LANES):
@@ -293,25 +297,49 @@
     return best
 
 
-def own_kernel(plan, own_ref, tags_ref, out_ref):
-    _, own_tags = tail_of(plan, own_ref)
+def own_kernel(plan, front_ref, back_ref, tags_ref, out_ref):
+    _, tags = tail_of(plan, front_ref)
+    own = (front_ref, back_ref)
+    rest = plan.capacity - plan.front
     for start in range(0, plan.capacity, plan.step):
         best = jnp.full((plan.step, LANES), -1.0, F32)
-        best = score_block(plan, own_ref, tags_ref, own_ref, own_tags, start, best, True)
+        best = score_block(
+            plan, own, tags_ref, front_ref, plan.front, 0, tags, start, best, True
+        )
+        best = score_block(
+            plan, own, tags_ref, back_ref, rest, plan.front, tags, start, best, True
+        )
         out_ref[pl.ds(start, plan.step), :] = best
 
 
-def other_kernel(plan, pos_ref, own_ref, tags_ref, other_ref, part_ref, out_ref):
-    own_note, _ = tail_of(plan, own_ref)
+def first_kernel(plan, front_ref, back_ref, tags_ref, other_ref, part_ref, out_ref):
+    _, tags = tail_of(plan, other_ref)
+    own = (front_ref, back_ref)
+    for start in range(0, plan.capacity, plan.step):
+        best = part_ref[pl.ds(start, plan.step), :]
+        best = score_block(
+            plan, own, tags_ref, other_ref, plan.front, 0, tags, start, best, False
+        )
+        out_ref[pl.ds(start, plan.step), :] = best
+
+
+def other_kernel(
+    plan, pos_ref, front_ref, back_ref, tags_ref, other_ref, last_ref, part_ref, out_ref
+):
+    own_note, _ = tail_of(plan, front_ref)
     other_note, other_tags = tail_of(plan, other_ref)
     note_lane = iota((1, LANES), 1)
     differs = (note_lane >= 32) & (own_note != other_note)
     raised = jnp.where(note_lane == 0, jnp.maximum(own_note, other_note), 0.0)
     flag = jnp.max(jnp.where(differs, 1.0, raised), axis=1, keepdims=True)
     found = [jnp.zeros((8, plan.chunk), F32)] * (plan.held // plan.chunk)
+    own = (front_ref, back_ref)
+    rest = plan.capacity - plan.front
     for start in range(0, plan.capacity, plan.step):
         best = part_ref[pl.ds(start, plan.step), :]
-        best = score_block(plan, own_ref, tags_ref, other_ref, other_tags, start, best, False)
+        best = score_block(
+            plan, own, tags_ref, last_ref, rest, plan.front, other_tags, start, best, False
+        )
         top = jnp.max(best, axis=1, keepdims=True)
         row = iota((plan.step, plan.chunk), 0) + start
         for index in range(plan.reach(start) // plan.chunk, plan.held // plan.chunk):
@@ -389,44 +417,60 @@
         ],
     )(cluster_ids.reshape(1, ROWS), embeddings)
     held = swap(plan, message)
-    packed, tags, pos = call(
+    front, rear, tags, pos = call(
         compact_kernel,
         plan,
         "compact",
         out_shape=(
-            shape((plan.capacity + plan.tail, WIDTH), BF16),
+            shape((plan.front + plan.tail, WIDTH), BF16),
+            shape((plan.capacity - plan.front, WIDTH), BF16),
             shape((plan.capacity, LANES), BF16),
             shape((8, plan.held), I32),
         ),
         in_specs=[VMEM],
-        out_specs=(VMEM, VMEM, VMEM),
+        out_specs=(VMEM,) * 4,
         scratch_shapes=[
             pltpu.VMEM((plan.held + plan.window, WIDTH), BF16),
             pltpu.VMEM((plan.held + plan.window, LANES), BF16),
         ],
     )(held)
-    other = lax.ppermute(packed, "core", [(0, 1), (1, 0)])
+    pairs = [(0, 1), (1, 0)]
+    other_front = lax.ppermute(front, "core", pairs)
+    other_rear = lax.ppermute(rear, "core", pairs)
     part = call(
         own_kernel,
         plan,
         "score_own",
         out_shape=shape((plan.capacity, LANES), F32),
-        in_specs=[VMEM, VMEM],
+        in_specs=[VMEM] * 3,
         out_specs=VMEM,
         cost_estimate=pl.CostEstimate(
             flops=2 * plan.capacity**2 * WIDTH,
             bytes_accessed=2 * plan.capacity * WIDTH,
             transcendentals=0,
         ),
-    )(packed, tags)
+    )(front, rear, tags)
+    part = call(
+        first_kernel,
+        plan,
+        "score_first",
+        out_shape=shape((plan.capacity, LANES), F32),
+        in_specs=[VMEM] * 5,
+        out_specs=VMEM,
+        cost_estimate=pl.CostEstimate(
+            flops=2 * plan.capacity * plan.front * WIDTH,
+            bytes_accessed=2 * plan.capacity * WIDTH,
+            transcendentals=0,
+        ),
+    )(front, rear, tags, other_front, part)
     best = call(
         other_kernel,
         plan,
         "score_other",
         out_shape=shape((CHIPS, LANES), F32),
-        in_specs=[VMEM] * 5,
+        in_specs=[VMEM] * 7,
         out_specs=VMEM,
-    )(pos, packed, tags, other, part)
+    )(pos, front, rear, tags, other_front, other_rear, part)
     back = swap(plan, best)
     answer, flag = call(
         answer_kernel,

time: 70.4 us -> 70.1 us (level)
  waiting for transfers between devices: 1.73 us -> 0.66 us
    ppermute x1 -> x2, waiting for transfers between devices: 1.73 us -> 0.66 us  [the longest x1 0.66 us: owner_path(): other_front = lax.ppermute(front, 'core', pairs)]
    pallas_call x1 -> x2, Pallas kernels: 1.72 us -> 2.56 us  [the longest x1 1.74 us: owner_path(): call(compact_kernel, plan, 'compact', out_shape=(shape((plan.front + plan...]
  transfers between devices with their start and end apart: 1 -> 2, of which waited for: 1 -> 1; matrix products, arithmetic and copies ran while one was open for 0% -> 0% of each run, Pallas kernels for 2% -> 3%
where the time goes in v6:
time: 70.1 us; the launch traced here: 69.9 us
  blocking collectives  58.7 us (84%)
  Pallas kernels  8.84 us (13%)
  loops' own time  0.86 us (1%)
    all_to_all x2, blocking collectives, swap(): lax.all_to_all(message, ('yx', 'z'), split_axis=0, concat_axis=0, tiled=T...  58.7 us
    pallas_call x1, Pallas kernels, owner_path(): call(send_kernel, plan, 'send', out_shape=(shape((plan.held, WIDTH), BF16...  3.27 us
    pallas_call x1, Pallas kernels, owner_path(): call(compact_kernel, plan, 'compact', out_shape=(shape((plan.front + plan...  1.74 us
  transfers between devices with their start and end apart: 2, of which 1 were waited for; matrix products, arithmetic and copies ran while one was open for 0% of the time, Pallas kernels for 3%

profile of v6, /device:TPU:0, one launch (start us, length us, event | category | flops | bytes accessed | tf_op | source)
XLA Modules:
  0.0 69.9 jit_solution(1193531134471636821)
XLA Ops:
  0.0 3.3 %send.3 = (bf16[1536,768]{1,0:T(8,128)(2,1)S(1)}, s32[8,512]{1,0:T(8,128)S(1)}) custom-call(s32[1,512]{1,0:T(1,128)} %bitcast.14.ids_ref, bf16[512,768]{1,0:T(8,128)(2,1)} %rows_ref.1), custom_call_target="tpu_custom_call" | custom-call | tf_op jit(solution)/shard_map/send/pallas_call | solution.py:406
  3.3 44.3 %all_to_all.68 = bf16[64,24,768]{2,1,0:T(8,128)(2,1)S(1)} all-to-all(bf16[64,24,768]{2,1,0:T(8,128)(2,1)S(1)} %bitcast.84), channel_id=1, replica_groups=mesh['yx'=16,'core'=2,'z'=4] {'yx','z'}, dimensions={0} | all-to-all | bytes 4718592 | tf_op jit(solution)/shard_map/all_to_all | solution.py:402
  47.6 1.7 %compact.3 = (bf16[528,768]{1,0:T(8,128)(2,1)S(1)}, bf16[256,768]{1,0:T(8,128)(2,1)S(1)}, bf16[768,128]{1,0:T(8,128)(2,1)S(1)}, s32[8,1536]{1,0:T(8,128)S(1)}) custom-call(bf16[1536,768]{1,0:T(8,128)(2,1)S(1)} %bitcast.82), custom_call_target="tpu_custom_call" | custom-call | tf_op jit(solution)/shard_map/compact/pallas_call | solution.py:420
  49.4 0.1 collective-permute-start.2
  49.5 0.5 collective-permute-start.3
  50.0 1.1 %score_own.3.part_ref = f32[768,128]{1,0:T(8,128)S(1)} custom-call(bf16[528,768]{1,0:T(8,128)(2,1)S(1)} %get-tuple-element.114.front_ref, bf16[256,768]{1,0:T(8,128)(2,1)S(1)} %get-tuple-element.115.back_ref, bf16[768,128]{1,0:T(8,128)(2,1)S(1)} %get-tuple-element.116.tags_ref), custom_call_target="tpu_custom_call" | custom-call | flops 905969664 | bytes 1179648 | tf_op jit(solution)/shard_map/score_own/pallas_call | solution.py:440
  51.2 0.7 collective-permute-done.2.other_ref
  51.8 0.8 %score_first.3.part_ref = f32[768,128]{1,0:T(8,128)S(1)} custom-call(bf16[528,768]{1,0:T(8,128)(2,1)S(1)} %get-tuple-element.114.front_ref, bf16[256,768]{1,0:T(8,128)(2,1)S(1)} %get-tuple-element.115.back_ref, bf16[768,128]{1,0:T(8,128)(2,1)S(1)} %get-tuple-element.116.tags_ref, bf16[528,768]{1,0:T(8,128)(2,1)S(1)} %collective-permute-done.2.other_ref, ...), custom_call_target="tpu_custom_call" | custom-call | flops 603979776 | bytes 1179648 | tf_op jit(solution)/shard_map/score_first/pallas_call | solution.py:453
  52.6 0.0 collective-permute-done.3.last_ref
  52.6 1.0 %score_other.3 = f32[64,128]{1,0:T(8,128)S(1)} custom-call(s32[8,1536]{1,0:T(8,128)S(1)} %get-tuple-element.113.pos_ref, bf16[528,768]{1,0:T(8,128)(2,1)S(1)} %get-tuple-element.114.front_ref, bf16[256,768]{1,0:T(8,128)(2,1)S(1)} %get-tuple-element.115.back_ref, bf16[768,128]{1,0:T(8,128)(2,1)S(1)} %get-tuple-element.116.tags_ref, ...), custom_call_target="tpu_custom_call" | custom-call | tf_op jit(solution)/shard_map/score_other/pallas_call | solution.py:466
  53.6 14.4 %all_to_all.69 = f32[64,1,128]{2,1,0:T(1,128)S(1)} all-to-all(f32[64,1,128]{2,1,0:T(1,128)S(1)} %bitcast.85), channel_id=1, replica_groups=mesh['yx'=16,'core'=2,'z'=4] {'yx','z'}, dimensions={0} | all-to-all | bytes 65536 | tf_op jit(solution)/shard_map/all_to_all | solution.py:402
  68.0 0.9 %answer.3 = (f32[1,512]{1,0:T(1,128)}, s32[1]{0:T(128)}) custom-call(s32[8,512]{1,0:T(8,128)S(1)} %get-tuple-element.111.where_ref, f32[64,128]{1,0:T(8,128)S(1)} %bitcast.86), custom_call_target="tpu_custom_call" | custom-call | tf_op jit(solution)/shard_map/answer/pallas_call | solution.py:475
  68.9 0.9 %while.27 = (f32[512]{0:T(512)}, s32[]{:T(128)}, s32[512]{0:T(512)}, bf16[512,768]{1,0:T(8,128)(2,1)}) while((f32[512]{0:T(512)}, s32[]{:T(128)}, s32[512]{0:T(512)}, bf16[512,768]{1,0:T(8,128)(2,1)}) %tuple.52), condition=%region_12.13_spmd, body=%region_0.12_spmd | while | flops 12118243328 | bytes 97099008 | solution.py:558
Async XLA Ops:
  49.4 2.4 %collective-permute-start.2 = (bf16[528,768]{1,0:T(8,128)(2,1)S(1)}, bf16[528,768]{1,0:T(8,128)(2,1)S(1)}, u32[]{:S(2)}, u32[]{:S(2)}) collective-permute-start(bf16[528,768]{1,0:T(8,128)(2,1)S(1)} %get-tuple-element.114.front_ref), channel_id=1, source_target_pairs={{0,4},{4,0},{1,5},{5,1},{2,6},{6,2},{3,7},{7,3},{8,12},{12,8},{9,1... | collective-permute-start | bytes 2433032 | tf_op jit(solution)/shard_map/ppermute | solution.py:438
  49.5 3.1 %collective-permute-start.3 = (bf16[256,768]{1,0:T(8,128)(2,1)S(1)}, bf16[256,768]{1,0:T(8,128)(2,1)S(1)}, u32[]{:S(2)}, u32[]{:S(2)}) collective-permute-start(bf16[256,768]{1,0:T(8,128)(2,1)S(1)} %get-tuple-element.115.back_ref), channel_id=1, source_target_pairs={{0,4},{4,0},{1,5},{5,1},{2,6},{6,2},{3,7},{7,3},{8,12},{12,8},{9,1... | collective-permute-start | bytes 1179656 | tf_op jit(solution)/shard_map/ppermute | solution.py:439

commit v7 on v5

--- a/solution.py
+++ b/solution.py
@@ -98,11 +98,12 @@
     ahead = (theirs > mine) | ((theirs == mine) & (index_row < index))
     order = jnp.sum(ahead.astype(F32), axis=1, keepdims=True).astype(I32)
     coded = jnp.where(mine >= 3, 1.0, 0.0) + jnp.where(mine >= 2, 64.0, 0.0)
-    coded = jnp.sum(coded + jnp.where(mine >= 1, 4096.0, 0.0)).astype(I32)
+    coded = coded + jnp.where(mine >= 1, 4096.0, 0.0)
+    coded = jnp.sum(coded, axis=0, keepdims=True).astype(I32)[0, 0]
     ends = [coded & 63, (coded >> 6) & 63, coded >> 12]
-    loads = [jnp.int32(0), jnp.int32(0), jnp.int32(0), jnp.int32(HEAVY_LOAD)]
-    taken = [jnp.int32(0), jnp.int32(0), jnp.int32(0), jnp.int32(1)]
-    code = jnp.full((GROUPS, 1), 3 * 32, I32)
+    states = [jnp.int32(kind) for kind in range(KINDS - 1)]
+    states.append(jnp.int32((HEAVY_LOAD << 8) + (1 << 2) + KINDS - 1))
+    picked = jnp.full((GROUPS, 1), KINDS - 1, I32)
     for turn in range(GROUPS - 1):
         if plan.sized:
             weight = jnp.where(
@@ -110,19 +111,13 @@
             )
         else:
             weight = jnp.int32(14)
-        first = loads[1] < loads[0]
-        last = loads[3] < loads[2]
-        low = jnp.where(first, loads[1], loads[0])
-        high = jnp.where(last, loads[3], loads[2])
-        kind = jnp.where(high < low, jnp.where(last, 3, 2), jnp.where(first, 1, 0))
-        place = taken[0]
-        for other in range(1, KINDS):
-            place = jnp.where(kind == other, taken[other], place)
-        for other in range(KINDS):
-            chosen = kind == other
-            loads[other] = loads[other] + jnp.where(chosen, weight, 0)
-            taken[other] = taken[other] + jnp.where(chosen, 1, 0)
-        code = jnp.where(order == turn, kind * 32 + place, code)
+        least = jnp.minimum(
+            jnp.minimum(states[0], states[1]), jnp.minimum(states[2], states[3])
+        )
+        step = (weight << 8) + (1 << 2)
+        states = [jnp.where(state == least, state + step, state) for state in states]
+        picked = jnp.where(order == turn, least, picked)
+    code = (picked & 3) * 32 + ((picked >> 2) & 63)
     return code, unsure
 
 

time: 70.4 us -> 70.2 us (level)
  no operation moved by 1% of the time
where the time goes in v7:
time: 70.2 us; the launch traced here: 70 us
  blocking collectives  58.7 us (84%)
  Pallas kernels  8.28 us (12%)
  waiting for transfers between devices  1.74 us (2%)
  loops' own time  0.86 us (1%)
    all_to_all x2, blocking collectives, swap(): lax.all_to_all(message, ('yx', 'z'), split_axis=0, concat_axis=0, tiled=T...  58.7 us
    pallas_call x1, Pallas kernels, owner_path(): call(send_kernel, plan, 'send', out_shape=(shape((plan.held, WIDTH), BF16...  3.02 us
    pallas_call x1, Pallas kernels, owner_path(): call(compact_kernel, plan, 'compact', out_shape=(shape((plan.capacity + p...  1.75 us
    ppermute x1, waiting for transfers between devices, owner_path(): other = lax.ppermute(packed, 'core', [(0, 1), (1, 0)])  1.74 us
    pallas_call x1, Pallas kernels, owner_path(): call(other_kernel, plan, 'score_other', out_shape=shape((CHIPS, LANES), F...  1.5 us
  transfers between devices with their start and end apart: 1, of which 1 were waited for; matrix products, arithmetic and copies ran while one was open for 0% of the time, Pallas kernels for 2%

profile of v7, /device:TPU:0, one launch (start us, length us, event | category | flops | bytes accessed | tf_op | source)
XLA Modules:
  0.0 70.0 jit_solution(4621479046308746554)
XLA Ops:
  0.0 3.0 %send.3 = (bf16[1536,768]{1,0:T(8,128)(2,1)S(1)}, s32[8,512]{1,0:T(8,128)S(1)}) custom-call(s32[1,512]{1,0:T(1,128)} %bitcast.14.ids_ref, bf16[512,768]{1,0:T(8,128)(2,1)} %rows_ref.1), custom_call_target="tpu_custom_call" | custom-call | tf_op jit(solution)/shard_map/send/pallas_call | solution.py:373
  3.0 44.3 %all_to_all.68 = bf16[64,24,768]{2,1,0:T(8,128)(2,1)S(1)} all-to-all(bf16[64,24,768]{2,1,0:T(8,128)(2,1)S(1)} %bitcast.84), channel_id=1, replica_groups=mesh['yx'=16,'core'=2,'z'=4] {'yx','z'}, dimensions={0} | all-to-all | bytes 4718592 | tf_op jit(solution)/shard_map/all_to_all | solution.py:369
  47.3 1.8 %compact.3 = (bf16[784,768]{1,0:T(8,128)(2,1)S(1)}, bf16[768,128]{1,0:T(8,128)(2,1)S(1)}, s32[8,1536]{1,0:T(8,128)S(1)}) custom-call(bf16[1536,768]{1,0:T(8,128)(2,1)S(1)} %bitcast.82), custom_call_target="tpu_custom_call" | custom-call | tf_op jit(solution)/shard_map/compact/pallas_call | solution.py:387
  49.2 0.1 collective-permute-start.1
  49.3 1.1 %score_own.3.part_ref = f32[768,128]{1,0:T(8,128)S(1)} custom-call(bf16[784,768]{1,0:T(8,128)(2,1)S(1)} %get-tuple-element.112.own_ref, bf16[768,128]{1,0:T(8,128)(2,1)S(1)} %get-tuple-element.113.tags_ref), custom_call_target="tpu_custom_call" | custom-call | flops 905969664 | bytes 1179648 | tf_op jit(solution)/shard_map/score_own/pallas_call | solution.py:404
  50.4 1.7 %collective-permute-done.1.other_ref = bf16[784,768]{1,0:T(8,128)(2,1)S(1)} collective-permute-done((bf16[784,768]{1,0:T(8,128)(2,1)S(1)}, bf16[784,768]{1,0:T(8,128)(2,1)S(1)}, u32[]{:S(2)}, u32[]{:S(2)}) %collective-permute-start.1) | collective-permute-done | bytes 1204256 | tf_op jit(solution)/shard_map/ppermute | solution.py:403
  52.1 1.5 %score_other.3 = f32[64,128]{1,0:T(8,128)S(1)} custom-call(s32[8,1536]{1,0:T(8,128)S(1)} %get-tuple-element.111.pos_ref, bf16[784,768]{1,0:T(8,128)(2,1)S(1)} %get-tuple-element.112.own_ref, bf16[768,128]{1,0:T(8,128)(2,1)S(1)} %get-tuple-element.113.tags_ref, bf16[784,768]{1,0:T(8,128)(2,1)S(1)} %collective-permute-done.1.other_ref, ...), custom_call_target="tpu_custom_call" | custom-call | tf_op jit(solution)/shard_map/score_other/pallas_call | solution.py:417
  53.6 14.4 %all_to_all.69 = f32[64,1,128]{2,1,0:T(1,128)S(1)} all-to-all(f32[64,1,128]{2,1,0:T(1,128)S(1)} %bitcast.85), channel_id=1, replica_groups=mesh['yx'=16,'core'=2,'z'=4] {'yx','z'}, dimensions={0} | all-to-all | bytes 65536 | tf_op jit(solution)/shard_map/all_to_all | solution.py:369
  68.0 0.9 %answer.3 = (f32[1,512]{1,0:T(1,128)}, s32[1]{0:T(128)}) custom-call(s32[8,512]{1,0:T(8,128)S(1)} %get-tuple-element.109.where_ref, f32[64,128]{1,0:T(8,128)S(1)} %bitcast.86), custom_call_target="tpu_custom_call" | custom-call | tf_op jit(solution)/shard_map/answer/pallas_call | solution.py:426
  68.9 0.9 %while.27 = (f32[512]{0:T(512)}, s32[]{:T(128)}, s32[512]{0:T(512)}, bf16[512,768]{1,0:T(8,128)(2,1)}) while((f32[512]{0:T(512)}, s32[]{:T(128)}, s32[512]{0:T(512)}, bf16[512,768]{1,0:T(8,128)(2,1)}) %tuple.52), condition=%region_12.13_spmd, body=%region_0.12_spmd | while | flops 10608293888 | bytes 95132888 | solution.py:509
Async XLA Ops:
  49.2 3.0 %collective-permute-start.1 = (bf16[784,768]{1,0:T(8,128)(2,1)S(1)}, bf16[784,768]{1,0:T(8,128)(2,1)S(1)}, u32[]{:S(2)}, u32[]{:S(2)}) collective-permute-start(bf16[784,768]{1,0:T(8,128)(2,1)S(1)} %get-tuple-element.112.own_ref), channel_id=1, source_target_pairs={{0,4},{4,0},{1,5},{5,1},{2,6},{6,2},{3,7},{7,3},{8,12},{12,8},{9,1... | collective-permute-start | bytes 3612680 | tf_op jit(solution)/shard_map/ppermute | solution.py:403
